TPU v7x, 32 devices: a whole 2x2x4 slice. The times are simulated.
32 devices in a mesh: lat: 8 (over y, x, core), freq: 4 (over z).
Axes of the slice: x: 2, y: 2, z: 4, core: 2. Of those that a mesh axis runs over, the one named last changes fastest.
Arguments:
- gravity: float32 [128, 21600], P('lat', 'freq'), may hold values from -6 to 6
- coef: bfloat16 [2176, 2, 2176], P(('lat', 'freq')), may hold values from -0.125 to 0.125
- legendre: bfloat16 [2176, 2176, 128], P(('lat', 'freq')), may hold values from -6 to 6
- order_table: int32 [2176], replicated, may hold values from 0 to 2175, as said below
- band_rows: int32 [128], P('lat'), may hold values from 0 to 2399, as said below
- kernel: bfloat16 [255, 10800], P(None, 'freq'), may hold values from -0.5 to 0.5
Outputs:
- geoid: float32 [128, 21600], P('lat', 'freq')
Inputs may be any that keep to these rules, and one draw needn't show every extreme that they name: `order_table`: A permutation of the orders 0 to 2175; the slot s lies in the block of slots s // 68, and its order m has m % 4 == (s // 68) % 4. `band_rows`: strictly increasing; the first row is parallel 0 and the last is parallel 2400 - 1.
All inputs are finite; a program needn't handle non-finite values.
Results may differ from a plain program's by a relative error of at most 0.0032.
Values may be sent and summed in bfloat16 or wider, within the bound.
A program may use at most 128 MiB of HBM per device.

v0:
```python
import jax
import jax.numpy as jnp
import numpy as np
from jax import lax
from jax.experimental import pallas as pl
from jax.experimental.pallas import tpu as pltpu
from jax.sharding import PartitionSpec as P

L = 21600
PA = 144
PB = 150
PH = 75


highest = lax.Precision.HIGHEST


def angle_table(first, second, period):
    phase = first * second % period
    return phase.astype(jnp.float32) * (2.0 * np.pi / period)


def forward_bands(grid, first_start, bands):
    rows = grid.shape[0]
    count_one = grid.shape[1]
    first_index = first_start + jnp.arange(count_one, dtype=jnp.int32)
    freq_one = jnp.arange(PA, dtype=jnp.int32)
    theta_one = angle_table(first_index[:, None], freq_one[None, :], PA)
    section_re = jnp.einsum("rab,ak->rbk", grid, jnp.cos(theta_one), precision=highest)
    section_im = -jnp.einsum("rab,ak->rbk", grid, jnp.sin(theta_one), precision=highest)
    second_index = jnp.arange(PB, dtype=jnp.int32)
    twist = angle_table(second_index[:, None], freq_one[None, :], L)
    twist_cos = jnp.cos(twist)
    twist_sin = jnp.sin(twist)
    turned_re = section_re * twist_cos + section_im * twist_sin
    turned_im = section_im * twist_cos - section_re * twist_sin
    freq_two = jnp.arange(PH, dtype=jnp.int32)
    theta_two = angle_table(second_index[:, None], freq_two[None, :], PB)
    cos_two = jnp.cos(theta_two)
    sin_two = jnp.sin(theta_two)
    spec_re = jnp.einsum("rbk,bm->rkm", turned_re, cos_two, precision=highest) + jnp.einsum(
        "rbk,bm->rkm", turned_im, sin_two, precision=highest
    )
    spec_im = jnp.einsum("rbk,bm->rkm", turned_im, cos_two, precision=highest) - jnp.einsum(
        "rbk,bm->rkm", turned_re, sin_two, precision=highest
    )
    scale = (2.0 / L) ** 0.5
    stacked = jnp.stack([spec_re, spec_im]) * scale
    span = PA // bands
    stacked = stacked.reshape(2, rows, span, bands, PH).transpose(3, 1, 0, 4, 2)
    return stacked.reshape(bands, rows, 2, PH * span)


def inverse_rows(spectra, band_ids, bands):
    count = spectra.shape[0]
    rows = spectra.shape[1]
    span = PA // bands
    parts = spectra.reshape(count, rows, 2, PH, span)
    part_re = parts[:, :, 0]
    part_im = parts[:, :, 1]
    freq_two = jnp.arange(PH, dtype=jnp.int32)
    second_index = jnp.arange(PB, dtype=jnp.int32)
    theta_two = angle_table(freq_two[:, None], second_index[None, :], PB)
    cos_two = jnp.cos(theta_two)
    sin_two = jnp.sin(theta_two)
    middle_re = jnp.einsum("brms,mn->brsn", part_re, cos_two, precision=highest) - jnp.einsum(
        "brms,mn->brsn", part_im, sin_two, precision=highest
    )
    middle_im = jnp.einsum("brms,mn->brsn", part_im, cos_two, precision=highest) + jnp.einsum(
        "brms,mn->brsn", part_re, sin_two, precision=highest
    )
    freq_one = jnp.arange(span, dtype=jnp.int32)[None, :] * bands + band_ids[:, None]
    twist = angle_table(freq_one[:, :, None], second_index[None, None, :], L)
    twist_cos = jnp.cos(twist)[:, None]
    twist_sin = jnp.sin(twist)[:, None]
    turned_re = middle_re * twist_cos - middle_im * twist_sin
    turned_im = middle_re * twist_sin + middle_im * twist_cos
    first_index = jnp.arange(PA, dtype=jnp.int32)
    theta_one = angle_table(freq_one[:, :, None], first_index[None, None, :], PA)
    grid = jnp.einsum(
        "brsn,bsa->ran", turned_re, jnp.cos(theta_one), precision=highest
    ) - jnp.einsum("brsn,bsa->ran", turned_im, jnp.sin(theta_one), precision=highest)
    return grid * (2.0 / L) ** 0.5


def general_device(gravity, coef, legendre, order_table, band_rows, kernel):
    bands = lax.axis_size("freq")
    blocks = lax.axis_size("lat")
    band_self = lax.axis_index("freq")
    block_self = lax.axis_index("lat")
    rows = gravity.shape[0]
    span = PA // bands
    local_grid = gravity.reshape(rows, span, PB)
    terms = forward_bands(local_grid, band_self * span, bands)
    observed = lax.psum_scatter(terms, "freq", scatter_dimension=0, tiled=True)[0]
    band_width = observed.shape[2]
    synth = jnp.einsum("ocn,onq->ocq", coef, legendre, preferred_element_type=jnp.float32).astype(
        jnp.bfloat16
    )
    routed = lax.all_to_all(synth, "lat", split_axis=2, concat_axis=0, tiled=True)
    per_slot = coef.shape[0]
    slot_ids = (
        (jnp.arange(blocks, dtype=jnp.int32)[:, None] * bands + band_self) * per_slot
        + jnp.arange(per_slot, dtype=jnp.int32)[None, :]
    ).reshape(-1)
    positions = order_table[slot_ids] // bands
    selector = (positions[:, None] == jnp.arange(band_width, dtype=jnp.int32)[None, :]).astype(
        jnp.bfloat16
    )
    model = jnp.einsum("jcr,jt->rct", routed, selector, preferred_element_type=jnp.float32)
    weight = jnp.cos((20.0 + band_rows.astype(jnp.float32) / 60.0) * (np.pi / 180.0))
    weighted = ((observed - model) * weight[:, None, None]).astype(jnp.bfloat16)
    total_rows = rows * blocks
    padded_width = -(-band_width // blocks) * blocks
    padding_cols = padded_width - band_width
    slab_width = padded_width // blocks
    spread = jnp.pad(weighted, ((0, 0), (0, 0), (0, padding_cols)))
    columns = lax.all_to_all(spread, "lat", split_axis=2, concat_axis=0, tiled=True)
    kernel_padded = jnp.pad(kernel, ((0, 0), (0, padding_cols)))
    kernel_own = lax.dynamic_slice_in_dim(kernel_padded, block_self * slab_width, slab_width, 1)
    full_offsets = np.arange(total_rows)[None, :] - np.arange(total_rows)[:, None] + total_rows - 1
    toeplitz_full = kernel_own[full_offsets]
    summed = jnp.einsum("pqk,qck->pck", toeplitz_full, columns, preferred_element_type=jnp.float32)
    returned = lax.all_to_all(summed, "lat", split_axis=0, concat_axis=2, tiled=True)
    stokes = returned[:, :, :band_width]
    grid_terms = inverse_rows(stokes[None], jnp.reshape(band_self, (1,)), bands)
    geoid = lax.psum_scatter(grid_terms, "freq", scatter_dimension=1, tiled=True)
    return geoid.reshape(rows, span * PB)


NA = 45
NC = 120
AP = 48
HALF = 64
CP = 128
SCALE = (2.0 / L) ** 0.5
SHIFT = 2.0**-7


def split_pair(values):
    high = values.astype(jnp.bfloat16)
    low = (values - high.astype(jnp.float32)).astype(jnp.bfloat16)
    return high, low


def numpy_pair(values):
    high = np.asarray(values, np.float32).astype(jnp.bfloat16)
    low = (values - high.astype(np.float64)).astype(jnp.bfloat16)
    return high, low


def tables():
    a = np.arange(NA)
    c = np.arange(NC)
    j1 = np.arange(NA)
    j2 = np.arange(NC // 2)
    first = np.zeros((4, CP, 2 * AP))
    twist = np.zeros((4, 2, HALF, CP))
    for b in range(4):
        theta = 2 * np.pi * (np.outer(4 * j1 + b, a) % (4 * NA)) / (4 * NA)
        first[b, :NA, :NA] = np.cos(theta)
        first[b, :NA, AP : AP + NA] = np.sin(theta)
        first[b, HALF : HALF + NA, :NA] = -np.sin(theta)
        first[b, HALF : HALF + NA, AP : AP + NA] = np.cos(theta)
        phi = 2 * np.pi * (np.outer(4 * j1 + b, c) % L) / L
        twist[b, 0, :NA, :NC] = np.cos(phi)
        twist[b, 1, :NA, :NC] = np.sin(phi)
    second = np.zeros((CP, CP))
    angle = 2 * np.pi * (np.outer(j2, c) % NC) / NC
    second[: NC // 2, :NC] = np.cos(angle)
    second[HALF : HALF + NC // 2, :NC] = np.sin(angle)
    return first, twist, second


def three_cols(values):
    high, low = numpy_pair(values)
    return np.concatenate([high, high, low], axis=-1)


def rows_of_three(values):
    high, low = split_pair(values)
    return jnp.concatenate([high, low, high], axis=0)


def cols_of_three(values):
    high, low = split_pair(values)
    return jnp.concatenate([high, low, high], axis=1)


def lane_sign():
    lane = lax.broadcasted_iota(jnp.int32, (1, CP), 1)
    return jnp.where(lane < HALF, 1.0, -1.0)


def forward_kernel(re_ref, im_ref, model_ref, weight_ref, first_ref, twist_ref, second_ref, out_ref, grid):
    band = lax.axis_index("freq")
    rows = re_ref.shape[0]
    grid[...] = jnp.zeros_like(grid)
    for a in range(NA):
        grid[:, a, :NC] = re_ref[:, a * NC : (a + 1) * NC]
        grid[:, AP + a, :NC] = im_ref[:, a * NC : (a + 1) * NC]
    first = first_ref[band]
    cosine = twist_ref[band, 0]
    sine = twist_ref[band, 1]
    second = second_ref[...]
    sign = lane_sign() * SCALE
    for r in range(rows):
        section = jnp.dot(first, rows_of_three(grid[r]), preferred_element_type=jnp.float32)
        top, bottom = section[:HALF], section[HALF:]
        turned = jnp.concatenate([top * cosine + bottom * sine, bottom * cosine - top * sine], axis=0)
        both = lax.dot_general(
            second, cols_of_three(turned), (((1,), (1,)), ((), ())), preferred_element_type=jnp.float32
        )
        spectrum = both[:HALF] * SCALE + pltpu.roll(both[HALF:], HALF, 1) * sign
        held = model_ref.shape[1]
        weight = weight_ref[r]
        out_ref[r, :held] = (spectrum[:held] - model_ref[r]) * weight
        out_ref[r, held:] = spectrum[held:] * weight


def inverse_kernel(in_ref, first_ref, twist_ref, second_ref, re_ref, own_ref, grid):
    band = lax.axis_index("freq")
    rows = in_ref.shape[0]
    first = first_ref[band]
    cosine = twist_ref[band, 0]
    sine = twist_ref[band, 1]
    second = second_ref[...]
    sign = lane_sign() * SCALE
    for r in range(rows):
        both = jnp.dot(second, rows_of_three(in_ref[r]), preferred_element_type=jnp.float32)
        middle = both[:CP] * SCALE - pltpu.roll(both[CP:], HALF, 1) * sign
        turned = middle * cosine + pltpu.roll(middle, HALF, 1) * sine
        grid[r] = lax.dot_general(
            first, cols_of_three(turned), (((1,), (1,)), ((), ())), preferred_element_type=jnp.float32
        )
    even = band % 2 == 0
    for a in range(NA):
        real = grid[:, a, :NC]
        re_ref[:, a * NC : (a + 1) * NC] = real
        own_ref[:, a * NC : (a + 1) * NC] = jnp.where(even, real, grid[:, AP + a, :NC])


def stokes_kernel(kernel_ref, weighted_ref, out_ref):
    total = weighted_ref.shape[0]
    pb, qb = 16, 8

    def p_step(i, carry):
        p0 = i * pb

        def q_step(j, acc):
            q0 = j * qb
            base = q0 - p0 + total - 1 - (pb - 1)
            window = [kernel_ref[base + d] for d in range(pb + qb - 1)]
            values = [weighted_ref[q0 + q].astype(jnp.float32) for q in range(qb)]
            acc = list(acc)
            for p in range(pb):
                for q in range(qb):
                    acc[p] = acc[p] + window[q - p + pb - 1] * values[q]
            return tuple(acc)

        zero = jnp.zeros(out_ref.shape[1:], jnp.float32)
        acc = lax.fori_loop(0, total // qb, q_step, (zero,) * pb)
        for p in range(pb):
            out_ref[p0 + p] = acc[p]
        return carry

    lax.fori_loop(0, total // pb, p_step, 0)


def swap(values, distance):
    return lax.ppermute(values, "freq", [(f, f ^ distance) for f in range(4)])


def pick(values, band):
    return jnp.asarray(values, jnp.float32)[band]


def band_device(gravity, coef, legendre, order_table, band_rows, kernel):
    band = lax.axis_index("freq")
    blocks = lax.axis_size("lat")
    block = lax.axis_index("lat")
    rows = gravity.shape[0]
    total = rows * blocks
    slots = coef.shape[0]
    deep = HALF // blocks
    first, twist, second = tables()
    vmem = pl.BlockSpec(memory_space=pltpu.VMEM)
    params = pltpu.CompilerParams(vmem_limit_bytes=48 * 2**20)

    even = band % 2 == 0
    lower = band < 2
    short = gravity.astype(jnp.float16)
    across = swap(short, 2).astype(jnp.float32)
    added = gravity + across
    taken = jnp.where(lower, gravity - across, across - gravity)
    beside = swap(jnp.where(even, taken, added).astype(jnp.float16), 1).astype(jnp.float32)
    h_re = jnp.where(even, added + jnp.where(lower, beside, -beside), beside)
    h_im = jnp.where(even, 0.0, jnp.where(lower, -taken, taken))

    synth = jnp.einsum("ocn,onq->ocq", coef, legendre, preferred_element_type=jnp.float32).astype(jnp.bfloat16)
    routed = lax.all_to_all(synth, "lat", split_axis=2, concat_axis=0, tiled=True)
    held = -(-(-(-order_table.shape[0] // 4) // NA) // 8) * 8
    mine = lax.dynamic_index_in_dim(order_table.reshape(blocks, 4, slots), band, 1, keepdims=False)
    place = mine.reshape(-1) // 4
    lane = place // NA * HALF + place % NA
    selector = (lane[:, None] == jnp.arange(held * HALF, dtype=jnp.int32)[None, :]).astype(jnp.bfloat16)
    model = jnp.einsum("jcr,jt->rct", routed, selector, preferred_element_type=jnp.float32)
    model = model.reshape(rows, 2, held, HALF).transpose(0, 2, 1, 3).reshape(rows, held, 2 * HALF)
    weight = jnp.cos((20.0 + band_rows.astype(jnp.float32) / 60.0) * (np.pi / 180.0))
    weight = jnp.broadcast_to(weight[:, None, None], (rows, 1, CP))

    forward_twist = twist.astype(np.float32)
    weighted = pl.pallas_call(
        forward_kernel,
        out_shape=jax.ShapeDtypeStruct((rows, HALF, CP), jnp.float32),
        in_specs=[vmem] * 7,
        out_specs=vmem,
        scratch_shapes=[pltpu.VMEM((rows, 2 * AP, CP), jnp.float32)],
        compiler_params=params,
        name="longitude_forward",
    )(h_re, h_im, model, weight, three_cols(first), forward_twist, three_cols(second))
    weighted = weighted.astype(jnp.bfloat16).reshape(rows, blocks, deep, CP)
    columns = lax.all_to_all(weighted, "lat", split_axis=1, concat_axis=0, tiled=True).reshape(total, deep, CP)

    width = deep * NA
    padded = jnp.pad(kernel, ((0, 0), (0, width * blocks - kernel.shape[1])))
    own = lax.dynamic_slice_in_dim(padded, block * width, width, 1).reshape(2 * total - 1, deep, NA)
    own = jnp.pad(own, ((0, 0), (0, 0), (0, HALF - NA)))
    own = jnp.concatenate([own, own], axis=2).astype(jnp.float32)
    summed = pl.pallas_call(
        stokes_kernel,
        out_shape=jax.ShapeDtypeStruct((total, deep, CP), jnp.float32),
        in_specs=[vmem] * 2,
        out_specs=vmem,
        compiler_params=params,
        name="stokes_rows",
    )(own, columns)
    returned = lax.all_to_all(summed.reshape(total, 1, deep, CP), "lat", split_axis=0, concat_axis=1, tiled=True)

    back_second = three_cols(np.concatenate([second[:HALF].T, second[HALF:].T], axis=0))
    turn = np.concatenate([twist[:, 0], twist[:, 0]], axis=1), np.concatenate([-twist[:, 1], twist[:, 1]], axis=1)
    back_twist = np.stack([turn[0].transpose(0, 2, 1), turn[1].transpose(0, 2, 1)], axis=1).astype(np.float32)
    back_first = three_cols(first.transpose(0, 2, 1))
    flat = jax.ShapeDtypeStruct(gravity.shape, jnp.float32)
    real, chosen = pl.pallas_call(
        inverse_kernel,
        out_shape=(flat, flat),
        in_specs=[vmem] * 4,
        out_specs=(vmem, vmem),
        scratch_shapes=[pltpu.VMEM((rows, 2 * AP, CP), jnp.float32)],
        compiler_params=params,
        name="longitude_inverse",
    )(returned.reshape(rows, HALF, CP), back_first, back_twist, back_second)

    beside = swap((real * SHIFT).astype(jnp.float16), 1).astype(jnp.float32) / SHIFT
    keep = pick([1, -1, 1, -1], band) * chosen + pick([1, 1, -1, -1], band) * beside
    give = chosen + pick([-1, 1, 1, -1], band) * beside
    return keep + swap((give * SHIFT).astype(jnp.float16), 2).astype(jnp.float32) / SHIFT


def fits(mesh):
    return mesh.shape["freq"] == 4 and HALF % mesh.shape["lat"] == 0


def solution(mesh):
    return jax.shard_map(
        band_device if fits(mesh) else general_device,
        mesh=mesh,
        in_specs=(
            P("lat", "freq"),
            P(("lat", "freq"), None, None),
            P(("lat", "freq"), None, None),
            P(),
            P("lat"),
            P(None, "freq"),
        ),
        out_specs=P("lat", "freq"),
        check_vma=False,
    )
```

profile of v0, /device:TPU:0, one launch (start us, length us, event | category | flops | bytes accessed | tf_op | source)
XLA Modules:
  0.0 87.2 jit_solution(8222791145500372964)
XLA Ops:
  0.0 1.1 %convert_element_type.42 = f16[16,5400]{1,0:T(8,128)(2,1)S(1)} convert(f32[16,5400]{1,0:T(8,128)} %param.15) | non-fusion elementwise | flops 86400 | bytes 518400 | tf_op jit(solution)/shard_map/convert_element_type | solution.py:292
  1.1 4.1 %collective-permute-start = (f16[16,5400]{1,0:T(8,128)(2,1)S(1)}, f16[16,5400]{1,0:T(8,128)(2,1)S(1)}, u32[]{:S(2)}, u32[]{:S(2)}) collective-permute-start(f16[16,5400]{1,0:T(8,128)(2,1)S(1)} %convert_element_type.42), channel_id=1, source_target_pairs={{0,2},{1,3},{2,0},{3,1},{4,6},{5,7},{6,4},{7,5},{8,10},{9,11},{10,... | collective-permute-start | bytes 518408 | tf_op jit(solution)/shard_map/ppermute | solution.py:271
  5.2 13.9 %convolution_convert_fusion = bf16[68,2,128]{2,1,0:T(2,128)(2,1)S(1)} fusion(bf16[68,2,2176]{2,1,0:T(2,128)(2,1)S(1)} %copy-done, bf16[68,2176,128]{2,1,0:T(8,128)(2,1)} %param.17), kind=kOutput, calls=%fused_computation.3 | convolution fusion | flops 75777024 | bytes 38506496 | tf_op jit(solution)/shard_map/ocn,onq->ocq/dot_general | solution.py:300
  19.1 0.8 copy.36
  19.9 3.7 %all-to-all-start = ((bf16[68,2,128]{0,1,2:T(2,128)(2,1)}), bf16[68,2,128]{0,1,2:T(2,128)(2,1)S(1)}, u32[]{:S(2)}, u32[]{:S(2)}) async-start(bf16[68,2,128]{0,1,2:T(2,128)(2,1)} %copy.36), calls=%async_computation | async-start | bytes 131072 | tf_op jit(solution)/shard_map/all_to_all | solution.py:301
  24.0 4.7 %all-to-all-done = bf16[68,2,128]{0,1,2:T(2,128)(2,1)S(1)} async-done(((bf16[68,2,128]{0,1,2:T(2,128)(2,1)}), bf16[68,2,128]{0,1,2:T(2,128)(2,1)S(1)}, u32[]{:S(2)}, u32[]{:S(2)}) %all-to-all-start) | async-done | bytes 34848 | tf_op jit(solution)/shard_map/all_to_all | solution.py:301
  28.9 1.6 %collective-permute-start.1 = (f16[16,5400]{1,0:T(8,128)(2,1)S(1)}, f16[16,5400]{1,0:T(8,128)(2,1)S(1)}, u32[]{:S(2)}, u32[]{:S(2)}) collective-permute-start(f16[16,5400]{1,0:T(8,128)(2,1)S(1)} %select_convert_fusion), channel_id=1, source_target_pairs={{0,1},{1,0},{2,3},{3,2},{4,5},{5,4},{6,7},{7,6},{8,9},{9,8},{10,11... | collective-permute-start | bytes 518408 | tf_op jit(solution)/shard_map/ppermute | solution.py:271
  30.6 0.5 fusion
  31.6 3.4 %collective-permute-done.1 = f16[16,5400]{1,0:T(8,128)(2,1)S(1)} collective-permute-done((f16[16,5400]{1,0:T(8,128)(2,1)S(1)}, f16[16,5400]{1,0:T(8,128)(2,1)S(1)}, u32[]{:S(2)}, u32[]{:S(2)}) %collective-permute-start.1) | collective-permute-done | bytes 172832 | tf_op jit(solution)/shard_map/ppermute | solution.py:271
  35.3 4.0 %longitude_forward.1 = f32[16,64,128]{2,1,0:T(8,128)S(1)} custom-call(f32[16,5400]{1,0:T(8,128)S(1)} %get-tuple-element.10.re_ref, f32[16,5400]{1,0:T(8,128)S(1)} %get-tuple-element.9.im_ref, f32[16,16,128]{2,1,0:T(8,128)S(1)} %reshape.83.model_ref, f32[16,1,128]{2,1,0:T(1,128)S(1)} %broadcast_in_dim.7.weight_ref, bf16[4,128,288]{2,1,0:T(8,128)(2,1)S(1)} %copy-done.2, ...), custom_call_target="tpu_custom_call" | custom-call | tf_op jit(solution)/shard_map/longitude_forward/pallas_call | solution.py:313
  39.4 0.8 copy.40
  40.1 3.4 %all-to-all-start.1 = ((bf16[16,8,8,128]{3,2,0,1:T(8,128)(2,1)}), bf16[16,8,8,128]{3,2,0,1:T(8,128)(2,1)S(1)}, u32[]{:S(2)}, u32[]{:S(2)}) async-start(bf16[16,8,8,128]{3,2,0,1:T(8,128)(2,1)} %copy.40), calls=%async_computation.1 | async-start | bytes 524288 | tf_op jit(solution)/shard_map/all_to_all | solution.py:323
  44.5 5.9 %all-to-all-done.1 = bf16[16,8,8,128]{3,2,0,1:T(8,128)(2,1)S(1)} async-done(((bf16[16,8,8,128]{3,2,0,1:T(8,128)(2,1)}), bf16[16,8,8,128]{3,2,0,1:T(8,128)(2,1)S(1)}, u32[]{:S(2)}, u32[]{:S(2)}) %all-to-all-start.1) | async-done | bytes 262176 | tf_op jit(solution)/shard_map/all_to_all | solution.py:323
  50.4 5.5 %stokes_rows.1 = f32[128,8,128]{2,1,0:T(8,128)S(1)} custom-call(f32[255,8,128]{2,1,0:T(8,128)S(1)} %maximum_convert_fusion.kernel_ref, bf16[128,8,128]{2,1,0:T(8,128)(2,1)S(1)} %bitcast.41), custom_call_target="tpu_custom_call" | custom-call | tf_op jit(solution)/shard_map/stokes_rows/pallas_call | solution.py:330
  56.0 12.3 %all_to_all.48 = f32[128,1,8,128]{3,2,1,0:T(8,128)S(1)} all-to-all(f32[128,1,8,128]{3,2,1,0:T(8,128)S(1)} %bitcast.40), channel_id=1, replica_groups=mesh['lat'=8,'freq'=4] {'lat'}, dimensions={0} | all-to-all | bytes 1048576 | tf_op jit(solution)/shard_map/all_to_all | solution.py:338
  68.3 2.3 %longitude_inverse.1 = (f32[16,5400]{1,0:T(8,128)S(1)}, f32[16,5400]{1,0:T(8,128)S(1)}) custom-call(f32[16,64,128]{2,1,0:T(8,128)S(1)} %bitcast.39, bf16[4,96,384]{2,1,0:T(8,128)(2,1)S(1)} %copy-done.3, f32[4,2,128,128]{3,2,1,0:T(8,128)S(1)} %copy-done.1, bf16[256,192]{1,0:T(8,128)(2,1)S(1)} %copy-done.5), custom_call_target="tpu_custom_call" | custom-call | tf_op jit(solution)/shard_map/longitude_inverse/pallas_call | solution.py:345
  70.7 1.7 %collective-permute-start.2 = (f16[16,5400]{1,0:T(8,128)(2,1)S(1)}, f16[16,5400]{1,0:T(8,128)(2,1)S(1)}, u32[]{:S(2)}, u32[]{:S(2)}) collective-permute-start(f16[16,5400]{1,0:T(8,128)(2,1)S(1)} %multiply_convert_fusion), channel_id=1, source_target_pairs={{0,1},{1,0},{2,3},{3,2},{4,5},{5,4},{6,7},{7,6},{8,9},{9,8},{10,11... | collective-permute-start | bytes 518408 | tf_op jit(solution)/shard_map/ppermute | solution.py:271
  72.3 0.6 dynamic_slice.20
  73.6 2.7 %collective-permute-done.2 = f16[16,5400]{1,0:T(8,128)(2,1)S(1)} collective-permute-done((f16[16,5400]{1,0:T(8,128)(2,1)S(1)}, f16[16,5400]{1,0:T(8,128)(2,1)S(1)}, u32[]{:S(2)}, u32[]{:S(2)}) %collective-permute-start.2) | collective-permute-done | bytes 172832 | tf_op jit(solution)/shard_map/ppermute | solution.py:271
  76.4 0.4 collective-permute-start.3
  76.8 0.6 dynamic_slice.19
  78.0 0.6 dynamic_slice.16
  78.6 7.1 %collective-permute-done.3 = f16[16,5400]{1,0:T(8,128)(2,1)S(1)} collective-permute-done((f16[16,5400]{1,0:T(8,128)(2,1)S(1)}, f16[16,5400]{1,0:T(8,128)(2,1)S(1)}, u32[]{:S(2)}, u32[]{:S(2)}) %collective-permute-start.3) | collective-permute-done | bytes 172832 | tf_op jit(solution)/shard_map/ppermute | solution.py:271
  85.7 1.5 %fusion.3 = f32[16,5400]{1,0:T(8,128)} fusion(f16[16,5400]{1,0:T(8,128)(2,1)S(1)} %collective-permute-done.2, f16[16,5400]{1,0:T(8,128)(2,1)S(1)} %collective-permute-done.3, f32[16,5400]{1,0:T(8,128)S(1)} %get-tuple-element.7, f32[]{:T(128)} %bitcast.15, f32[]{:T(128)} %bitcast), kind=kLoop, calls=%fused_computation.16 | loop fusion | flops 604800 | bytes 1036808 | tf_op jit(solution)/shard_map/add | solution.py:358
  (52 shorter events, 2.4 us)
Async XLA Ops:
  0.0 5.2 %copy-start = (bf16[68,2,2176]{2,1,0:T(2,128)(2,1)S(1)}, bf16[68,2,2176]{2,1,0:T(2,128)(2,1)}, u32[]{:S(2)}) copy-start(bf16[68,2,2176]{2,1,0:T(2,128)(2,1)} %param.16) | copy-start | bytes 1775620
  1.1 22.6 %copy-start.9 = (s32[2176]{0:T(1024)S(1)}, s32[2176]{0:T(1024)}, u32[]{:S(2)}) copy-start(s32[2176]{0:T(1024)} %param.18) | copy-start | bytes 26116
  1.1 22.8 %copy-start.10 = (s32[16]{0:T(128)S(1)}, s32[16]{0:T(128)}, u32[]{:S(2)}) copy-start(s32[16]{0:T(128)} %param.19) | copy-start | bytes 196
  1.1 27.7 %copy-start.7 = (f32[16,5400]{1,0:T(8,128)S(1)}, f32[16,5400]{1,0:T(8,128)}, u32[]{:S(2)}) copy-start(f32[16,5400]{1,0:T(8,128)} %param.15) | copy-start | bytes 1036804
  1.1 27.7 %collective-permute-start = (f16[16,5400]{1,0:T(8,128)(2,1)S(1)}, f16[16,5400]{1,0:T(8,128)(2,1)S(1)}, u32[]{:S(2)}, u32[]{:S(2)}) collective-permute-start(f16[16,5400]{1,0:T(8,128)(2,1)S(1)} %convert_element_type.42), channel_id=1, source_target_pairs={{0,2},{1,3},{2,0},{3,1},{4,6},{5,7},{6,4},{7,5},{8,10},{9,11},{10,... | collective-permute-start | bytes 518408 | tf_op jit(solution)/shard_map/ppermute | solution.py:271
  19.9 8.7 %all-to-all-start = ((bf16[68,2,128]{0,1,2:T(2,128)(2,1)}), bf16[68,2,128]{0,1,2:T(2,128)(2,1)S(1)}, u32[]{:S(2)}, u32[]{:S(2)}) async-start(bf16[68,2,128]{0,1,2:T(2,128)(2,1)} %copy.36), calls=%async_computation | async-start | bytes 131072 | tf_op jit(solution)/shard_map/all_to_all | solution.py:301
  23.9 11.3 %copy-start.2 = (bf16[4,128,288]{2,1,0:T(8,128)(2,1)S(1)}, bf16[4,128,288]{2,1,0:T(8,128)(2,1)}, u32[]{:S(2)}) copy-start(bf16[4,128,288]{2,1,0:T(8,128)(2,1)} %constant.99.clone.first_ref) | copy-start | bytes 884740
  24.0 11.3 %copy-start.4 = (f32[4,2,64,128]{3,2,1,0:T(8,128)S(1)}, f32[4,2,64,128]{3,2,1,0:T(8,128)}, u32[]{:S(2)}) copy-start(f32[4,2,64,128]{3,2,1,0:T(8,128)} %constant.100.clone.twist_ref) | copy-start | bytes 786436
  24.0 11.3 %copy-start.6 = (bf16[128,384]{1,0:T(8,128)(2,1)S(1)}, bf16[128,384]{1,0:T(8,128)(2,1)}, u32[]{:S(2)}) copy-start(bf16[128,384]{1,0:T(8,128)(2,1)} %constant.101.clone.second_ref) | copy-start | bytes 294916
  28.9 6.1 %collective-permute-start.1 = (f16[16,5400]{1,0:T(8,128)(2,1)S(1)}, f16[16,5400]{1,0:T(8,128)(2,1)S(1)}, u32[]{:S(2)}, u32[]{:S(2)}) collective-permute-start(f16[16,5400]{1,0:T(8,128)(2,1)S(1)} %select_convert_fusion), channel_id=1, source_target_pairs={{0,1},{1,0},{2,3},{3,2},{4,5},{5,4},{6,7},{7,6},{8,9},{9,8},{10,11... | collective-permute-start | bytes 518408 | tf_op jit(solution)/shard_map/ppermute | solution.py:271
  35.2 8.4 %copy-start.8 = (bf16[255,2700]{0,1:T(8,128)(2,1)S(1)}, bf16[255,2700]{0,1:T(8,128)(2,1)}, u32[]{:S(2)}) copy-start(bf16[255,2700]{0,1:T(8,128)(2,1)} %param.20) | copy-start | bytes 4131004
  40.1 10.3 %all-to-all-start.1 = ((bf16[16,8,8,128]{3,2,0,1:T(8,128)(2,1)}), bf16[16,8,8,128]{3,2,0,1:T(8,128)(2,1)S(1)}, u32[]{:S(2)}, u32[]{:S(2)}) async-start(bf16[16,8,8,128]{3,2,0,1:T(8,128)(2,1)} %copy.40), calls=%async_computation.1 | async-start | bytes 524288 | tf_op jit(solution)/shard_map/all_to_all | solution.py:323
  44.5 23.8 %copy-start.1 = (f32[4,2,128,128]{3,2,1,0:T(8,128)S(1)}, f32[4,2,128,128]{3,2,1,0:T(8,128)}, u32[]{:S(2)}) copy-start(f32[4,2,128,128]{3,2,1,0:T(8,128)} %constant.103.clone.twist_ref) | copy-start | bytes 1572868
  44.5 23.8 %copy-start.3 = (bf16[4,96,384]{2,1,0:T(8,128)(2,1)S(1)}, bf16[4,96,384]{2,1,0:T(8,128)(2,1)}, u32[]{:S(2)}) copy-start(bf16[4,96,384]{2,1,0:T(8,128)(2,1)} %constant.102.clone.first_ref) | copy-start | bytes 884740
  44.5 23.8 %copy-start.5 = (bf16[256,192]{1,0:T(8,128)(2,1)S(1)}, bf16[256,192]{1,0:T(8,128)(2,1)}, u32[]{:S(2)}) copy-start(bf16[256,192]{1,0:T(8,128)(2,1)} %constant.104.clone.second_ref) | copy-start | bytes 294916
  55.9 16.4 %copy-start.13 = (f32[4]{0:T(128)S(1)}, f32[4]{0:T(128)}, u32[]{:S(2)}) copy-start(f32[4]{0:T(128)} %constant.107.clone) | copy-start | bytes 52
  55.9 20.8 %copy-start.12 = (f32[4]{0:T(128)S(1)}, f32[4]{0:T(128)}, u32[]{:S(2)}) copy-start(f32[4]{0:T(128)} %constant.106.clone) | copy-start | bytes 52
  55.9 22.1 %copy-start.11 = (f32[4]{0:T(128)S(1)}, f32[4]{0:T(128)}, u32[]{:S(2)}) copy-start(f32[4]{0:T(128)} %constant.105.clone) | copy-start | bytes 52
  70.7 5.6 %collective-permute-start.2 = (f16[16,5400]{1,0:T(8,128)(2,1)S(1)}, f16[16,5400]{1,0:T(8,128)(2,1)S(1)}, u32[]{:S(2)}, u32[]{:S(2)}) collective-permute-start(f16[16,5400]{1,0:T(8,128)(2,1)S(1)} %multiply_convert_fusion), channel_id=1, source_target_pairs={{0,1},{1,0},{2,3},{3,2},{4,5},{5,4},{6,7},{7,6},{8,9},{9,8},{10,11... | collective-permute-start | bytes 518408 | tf_op jit(solution)/shard_map/ppermute | solution.py:271
  76.4 9.4 %collective-permute-start.3 = (f16[16,5400]{1,0:T(8,128)(2,1)S(1)}, f16[16,5400]{1,0:T(8,128)(2,1)S(1)}, u32[]{:S(2)}, u32[]{:S(2)}) collective-permute-start(f16[16,5400]{1,0:T(8,128)(2,1)S(1)} %fusion.6), channel_id=1, source_target_pairs={{0,2},{1,3},{2,0},{3,1},{4,6},{5,7},{6,4},{7,5},{8,10},{9,11},{10,... | collective-permute-start | bytes 518408 | tf_op jit(solution)/shard_map/ppermute | solution.py:271
where the time goes:
time: 87.6 us; the launch traced here: 87.2 us
  waiting for transfers between devices  23.8 us (27%)
  starting transfers between devices  14.9 us (17%)
  matrix products  14.4 us (16%)
  blocking collectives  12.3 us (14%)
  Pallas kernels  11.8 us (13%)
  local copies, waits for them, and re-layouts  5 us (6%)
  other arithmetic  3.24 us (4%)
  between operations  1.67 us (2%)
    dot_general x1, matrix products, band_device(): jnp.einsum('ocn,onq->ocq', coef, legendre, preferred_element_type=jnp.flo...  13.9 us
    ppermute x4, waiting for transfers between devices, swap(): return lax.ppermute(values, 'freq', [(f, f ^ distance) for f in range(4)])  13.2 us
    all_to_all x1, blocking collectives, band_device(): lax.all_to_all(summed.reshape(total, 1, deep, CP), 'lat', split_axis=0, c...  12.3 us
    ppermute x4, starting transfers between devices, swap(): return lax.ppermute(values, 'freq', [(f, f ^ distance) for f in range(4)])  7.8 us
    all_to_all x1, waiting for transfers between devices, band_device(): lax.all_to_all(weighted, 'lat', split_axis=1, concat_axis=0, tiled=True)  5.87 us
    pallas_call x1, Pallas kernels, band_device(): pl.pallas_call(stokes_kernel, out_shape=jax.ShapeDtypeStruct((total, deep...  5.5 us
    all_to_all x1, waiting for transfers between devices, band_device(): lax.all_to_all(synth, 'lat', split_axis=2, concat_axis=0, tiled=True)  4.66 us
    pallas_call x1, Pallas kernels, band_device(): pl.pallas_call(forward_kernel, out_shape=jax.ShapeDtypeStruct((rows, HALF...  4.04 us
  transfers between devices with their start and end apart: 6, of which 5 were waited for; matrix products, arithmetic and copies ran while one was open for 22% of the time, Pallas kernels for 0%

commit v1 on v0

--- a/solution.py
+++ b/solution.py
@@ -1,3 +1,5 @@
+import functools
+
 import jax
 import jax.numpy as jnp
 import numpy as np
@@ -192,9 +194,11 @@
     return jnp.where(lane < HALF, 1.0, -1.0)
 
 
-def forward_kernel(re_ref, im_ref, model_ref, weight_ref, first_ref, twist_ref, second_ref, out_ref, grid):
+def forward_kernel(re_ref, im_ref, model_ref, weight_ref, first_ref, twist_ref, second_ref, out_ref, grid, parts):
     band = lax.axis_index("freq")
     rows = re_ref.shape[0]
+    blocks = out_ref.shape[0]
+    deep = HALF // blocks
     grid[...] = jnp.zeros_like(grid)
     for a in range(NA):
         grid[:, a, :NC] = re_ref[:, a * NC : (a + 1) * NC]
@@ -214,20 +218,25 @@
         spectrum = both[:HALF] * SCALE + pltpu.roll(both[HALF:], HALF, 1) * sign
         held = model_ref.shape[1]
         weight = weight_ref[r]
-        out_ref[r, :held] = (spectrum[:held] - model_ref[r]) * weight
-        out_ref[r, held:] = spectrum[held:] * weight
-
-
-def inverse_kernel(in_ref, first_ref, twist_ref, second_ref, re_ref, own_ref, grid):
+        residual = jnp.concatenate([spectrum[:held] - model_ref[r], spectrum[held:]], axis=0) * weight
+        parts[:, r * deep : (r + 1) * deep] = residual.reshape(blocks, deep, CP)
+    out_ref[...] = parts[...].astype(out_ref.dtype)
+
+
+def inverse_kernel(start, in_ref, first_ref, twist_ref, second_ref, re_ref, own_ref, grid, wide):
     band = lax.axis_index("freq")
-    rows = in_ref.shape[0]
+    rows = re_ref.shape[0]
+    blocks = in_ref.shape[0]
+    deep = HALF // blocks
     first = first_ref[band]
     cosine = twist_ref[band, 0]
     sine = twist_ref[band, 1]
     second = second_ref[...]
     sign = lane_sign() * SCALE
+    wide[...] = in_ref[:, start * deep : (start + rows) * deep].astype(jnp.float32)
     for r in range(rows):
-        both = jnp.dot(second, rows_of_three(in_ref[r]), preferred_element_type=jnp.float32)
+        sums = wide[:, r * deep : (r + 1) * deep].reshape(HALF, CP).astype(jnp.bfloat16)
+        both = jnp.dot(second, jnp.concatenate([sums, sums], axis=0), preferred_element_type=jnp.float32)
         middle = both[:CP] * SCALE - pltpu.roll(both[CP:], HALF, 1) * sign
         turned = middle * cosine + pltpu.roll(middle, HALF, 1) * sine
         grid[r] = lax.dot_general(
@@ -240,9 +249,16 @@
         own_ref[:, a * NC : (a + 1) * NC] = jnp.where(even, real, grid[:, AP + a, :NC])
 
 
-def stokes_kernel(kernel_ref, weighted_ref, out_ref):
-    total = weighted_ref.shape[0]
+def stokes_kernel(kernel_ref, weighted_ref, out_ref, values, sums):
+    blocks = weighted_ref.shape[0]
+    total = values.shape[0]
+    deep = values.shape[1]
+    share = total // blocks
     pb, qb = 16, 8
+    for source in range(blocks):
+        values[source * share : (source + 1) * share] = (
+            weighted_ref[source].astype(jnp.float32).reshape(share, deep, CP)
+        )
 
     def p_step(i, carry):
         p0 = i * pb
@@ -251,28 +267,74 @@
             q0 = j * qb
             base = q0 - p0 + total - 1 - (pb - 1)
             window = [kernel_ref[base + d] for d in range(pb + qb - 1)]
-            values = [weighted_ref[q0 + q].astype(jnp.float32) for q in range(qb)]
+            terms = [values[q0 + q] for q in range(qb)]
             acc = list(acc)
             for p in range(pb):
                 for q in range(qb):
-                    acc[p] = acc[p] + window[q - p + pb - 1] * values[q]
+                    acc[p] = acc[p] + window[q - p + pb - 1] * terms[q]
             return tuple(acc)
 
-        zero = jnp.zeros(out_ref.shape[1:], jnp.float32)
+        zero = jnp.zeros(values.shape[1:], jnp.float32)
         acc = lax.fori_loop(0, total // qb, q_step, (zero,) * pb)
         for p in range(pb):
-            out_ref[p0 + p] = acc[p]
+            sums[p0 + p] = acc[p]
         return carry
 
     lax.fori_loop(0, total // pb, p_step, 0)
+    for target in range(blocks):
+        block = sums[target * share : (target + 1) * share].reshape(share * deep, CP)
+        out_ref[target] = block.astype(out_ref.dtype)
+
+
+def exchange_kernel(src, dst, send, recv, near):
+    me = lax.axis_index("lat")
+    count = src.shape[0]
+    peers = [lax.rem(me + d, count) for d in range(1, count)]
+    barrier = pltpu.get_barrier_semaphore()
+    for peer in peers:
+        pl.semaphore_signal(barrier, inc=1, device_id={"lat": peer}, device_id_type=pl.DeviceIdType.MESH)
+    pl.semaphore_wait(barrier, count - 1)
+    copies = []
+    for d, peer in enumerate(peers):
+        copy = pltpu.make_async_remote_copy(
+            src_ref=src.at[peer],
+            dst_ref=dst.at[me],
+            send_sem=send.at[d],
+            recv_sem=recv.at[d],
+            device_id={"lat": peer},
+            device_id_type=pl.DeviceIdType.MESH,
+        )
+        copy.start()
+        copies.append(copy)
+    own = pltpu.make_async_copy(src.at[me], dst.at[me], near)
+    own.start()
+    own.wait()
+    for copy in copies:
+        copy.wait()
+
+
+def exchange(values, number, name):
+    count = values.shape[0]
+    vmem = pl.BlockSpec(memory_space=pltpu.VMEM)
+    return pl.pallas_call(
+        exchange_kernel,
+        out_shape=jax.ShapeDtypeStruct(values.shape, values.dtype),
+        in_specs=[vmem],
+        out_specs=vmem,
+        scratch_shapes=[
+            pltpu.SemaphoreType.DMA((count - 1,)),
+            pltpu.SemaphoreType.DMA((count - 1,)),
+            pltpu.SemaphoreType.DMA,
+        ],
+        compiler_params=pltpu.CompilerParams(
+            collective_id=number, has_side_effects=True, vmem_limit_bytes=32 * 2**20
+        ),
+        name=name,
+    )(values)
 
 
 def swap(values, distance):
     return lax.ppermute(values, "freq", [(f, f ^ distance) for f in range(4)])
-
-
-def pick(values, band):
-    return jnp.asarray(values, jnp.float32)[band]
 
 
 def band_device(gravity, coef, legendre, order_table, band_rows, kernel):
@@ -298,29 +360,32 @@
     h_im = jnp.where(even, 0.0, jnp.where(lower, -taken, taken))
 
     synth = jnp.einsum("ocn,onq->ocq", coef, legendre, preferred_element_type=jnp.float32).astype(jnp.bfloat16)
-    routed = lax.all_to_all(synth, "lat", split_axis=2, concat_axis=0, tiled=True)
+    synth = synth.reshape(slots, 2, blocks, rows).transpose(2, 3, 1, 0).reshape(blocks, rows * 2, slots)
+    synth = jnp.pad(synth, ((0, 0), (0, 0), (0, CP - slots)))
+    routed = exchange(synth, 0, "route_synth")
     held = -(-(-(-order_table.shape[0] // 4) // NA) // 8) * 8
     mine = lax.dynamic_index_in_dim(order_table.reshape(blocks, 4, slots), band, 1, keepdims=False)
-    place = mine.reshape(-1) // 4
-    lane = place // NA * HALF + place % NA
-    selector = (lane[:, None] == jnp.arange(held * HALF, dtype=jnp.int32)[None, :]).astype(jnp.bfloat16)
-    model = jnp.einsum("jcr,jt->rct", routed, selector, preferred_element_type=jnp.float32)
+    place = mine // 4
+    lane = jnp.pad(place // NA * HALF + place % NA, ((0, 0), (0, CP - slots)), constant_values=-1)
+    selector = (lane[:, :, None] == jnp.arange(held * HALF, dtype=jnp.int32)).astype(jnp.bfloat16)
+    model = jnp.einsum("brs,bst->rt", routed, selector, preferred_element_type=jnp.float32)
     model = model.reshape(rows, 2, held, HALF).transpose(0, 2, 1, 3).reshape(rows, held, 2 * HALF)
     weight = jnp.cos((20.0 + band_rows.astype(jnp.float32) / 60.0) * (np.pi / 180.0))
     weight = jnp.broadcast_to(weight[:, None, None], (rows, 1, CP))
 
-    forward_twist = twist.astype(np.float32)
     weighted = pl.pallas_call(
         forward_kernel,
-        out_shape=jax.ShapeDtypeStruct((rows, HALF, CP), jnp.float32),
+        out_shape=jax.ShapeDtypeStruct((blocks, rows * deep, CP), jnp.bfloat16),
         in_specs=[vmem] * 7,
         out_specs=vmem,
-        scratch_shapes=[pltpu.VMEM((rows, 2 * AP, CP), jnp.float32)],
+        scratch_shapes=[
+            pltpu.VMEM((rows, 2 * AP, CP), jnp.float32),
+            pltpu.VMEM((blocks, rows * deep, CP), jnp.float32),
+        ],
         compiler_params=params,
         name="longitude_forward",
-    )(h_re, h_im, model, weight, three_cols(first), forward_twist, three_cols(second))
-    weighted = weighted.astype(jnp.bfloat16).reshape(rows, blocks, deep, CP)
-    columns = lax.all_to_all(weighted, "lat", split_axis=1, concat_axis=0, tiled=True).reshape(total, deep, CP)
+    )(h_re, h_im, model, weight, three_cols(first), twist.astype(np.float32), three_cols(second))
+    columns = exchange(weighted, 1, "send_columns")
 
     width = deep * NA
     padded = jnp.pad(kernel, ((0, 0), (0, width * blocks - kernel.shape[1])))
@@ -329,33 +394,43 @@
     own = jnp.concatenate([own, own], axis=2).astype(jnp.float32)
     summed = pl.pallas_call(
         stokes_kernel,
-        out_shape=jax.ShapeDtypeStruct((total, deep, CP), jnp.float32),
+        out_shape=jax.ShapeDtypeStruct((blocks, rows * deep, CP), jnp.bfloat16),
         in_specs=[vmem] * 2,
         out_specs=vmem,
+        scratch_shapes=[pltpu.VMEM((total, deep, CP), jnp.float32), pltpu.VMEM((total, deep, CP), jnp.float32)],
         compiler_params=params,
         name="stokes_rows",
     )(own, columns)
-    returned = lax.all_to_all(summed.reshape(total, 1, deep, CP), "lat", split_axis=0, concat_axis=1, tiled=True)
-
-    back_second = three_cols(np.concatenate([second[:HALF].T, second[HALF:].T], axis=0))
+    returned = exchange(summed, 2, "return_sums")
+
+    back_second = np.concatenate([second[:HALF].T, second[HALF:].T], axis=0)
+    back_second = np.concatenate(numpy_pair(back_second), axis=1)
     turn = np.concatenate([twist[:, 0], twist[:, 0]], axis=1), np.concatenate([-twist[:, 1], twist[:, 1]], axis=1)
     back_twist = np.stack([turn[0].transpose(0, 2, 1), turn[1].transpose(0, 2, 1)], axis=1).astype(np.float32)
     back_first = three_cols(first.transpose(0, 2, 1))
-    flat = jax.ShapeDtypeStruct(gravity.shape, jnp.float32)
-    real, chosen = pl.pallas_call(
-        inverse_kernel,
-        out_shape=(flat, flat),
-        in_specs=[vmem] * 4,
-        out_specs=(vmem, vmem),
-        scratch_shapes=[pltpu.VMEM((rows, 2 * AP, CP), jnp.float32)],
-        compiler_params=params,
-        name="longitude_inverse",
-    )(returned.reshape(rows, HALF, CP), back_first, back_twist, back_second)
-
-    beside = swap((real * SHIFT).astype(jnp.float16), 1).astype(jnp.float32) / SHIFT
-    keep = pick([1, -1, 1, -1], band) * chosen + pick([1, 1, -1, -1], band) * beside
-    give = chosen + pick([-1, 1, 1, -1], band) * beside
-    return keep + swap((give * SHIFT).astype(jnp.float16), 2).astype(jnp.float32) / SHIFT
+    keep_own = jnp.where(even | (band == 1), 1.0, -1.0) * jnp.where(band == 1, -1.0, 1.0)
+    keep_beside = jnp.where(lower, 1.0, -1.0)
+    give_beside = jnp.where((band == 1) | (band == 2), 1.0, -1.0)
+    part = rows // 2
+    flat = jax.ShapeDtypeStruct((part, gravity.shape[1]), jnp.float32)
+    pieces = []
+    for start in range(0, rows, part):
+        real, chosen = pl.pallas_call(
+            functools.partial(inverse_kernel, start),
+            out_shape=(flat, flat),
+            in_specs=[vmem] * 4,
+            out_specs=(vmem, vmem),
+            scratch_shapes=[
+                pltpu.VMEM((part, 2 * AP, CP), jnp.float32),
+                pltpu.VMEM((blocks, part * deep, CP), jnp.float32),
+            ],
+            compiler_params=params,
+            name="longitude_inverse",
+        )(returned, back_first, back_twist, back_second)
+        beside = swap((real * SHIFT).astype(jnp.float16), 1).astype(jnp.float32) / SHIFT
+        give = swap(((chosen + give_beside * beside) * SHIFT).astype(jnp.float16), 2)
+        pieces.append(keep_own * chosen + keep_beside * beside + give.astype(jnp.float32) / SHIFT)
+    return jnp.concatenate(pieces, axis=0)
 
 
 def fits(mesh):

time: 87.6 us -> 81.7 us (0.933)
  Pallas kernels: 11.8 us -> 34 us
  blocking collectives: 12.3 us -> 0 us
  waiting for transfers between devices: 23.8 us -> 11.9 us
  starting transfers between devices: 14.9 us -> 10 us
  matrix products: 14.4 us -> 16 us
  between operations: 1.67 us -> 0.3 us
  other arithmetic: 3.24 us -> 4.21 us
    pallas_call x3 -> x7, Pallas kernels: 11.8 us -> 34 us  [the longest x3 18.1 us: exchange(): pl.pallas_call(exchange_kernel, out_shape=jax.ShapeDtypeStruct(values.sha...]
    all_to_all x1 -> x0, blocking collectives: 12.3 us -> none  [band_device(): lax.all_to_all(summed.reshape(total, 1, deep, CP), 'lat', split_axis=0, c...]
    all_to_all x2 -> x0, waiting for transfers between devices: 10.5 us -> none  [the longest x1 5.87 us: band_device(): lax.all_to_all(weighted, 'lat', split_axis=1, concat_axis=0, tiled=True)]
    all_to_all x2 -> x0, starting transfers between devices: 7.14 us -> none  [the longest x1 3.72 us: band_device(): lax.all_to_all(synth, 'lat', split_axis=2, concat_axis=0, tiled=True)]
    ppermute x4 -> x6, starting transfers between devices: 7.8 us -> 10 us  [swap(): return lax.ppermute(values, 'freq', [(f, f ^ distance) for f in range(4)])]
    dynamic_slice x3 -> x0, local copies, waits for them, and re-layouts: 1.79 us -> none  [pick(): return jnp.asarray(values, jnp.float32)[band]]
    dot_general x0 -> x1, matrix products: none -> 1.57 us  [band_device(): jnp.einsum('brs,bst->rt', routed, selector, preferred_element_type=jnp.fl...]
    add x2 -> x3, other arithmetic: 1.48 us -> 0.12 us  [the longest x2 0.1 us: band_device(): keep_own * chosen + keep_beside * beside + give.astype(jnp.float32) / SHIFT]
  transfers between devices with their start and end apart: 6 -> 6, of which waited for: 5 -> 5; matrix products, arithmetic and copies ran while one was open for 22% -> 26% of each run, Pallas kernels for 0% -> 6%
where the time goes in v1:
time: 81.7 us; the launch traced here: 81.5 us
  Pallas kernels  34 us (42%)
  matrix products  16 us (20%)
  waiting for transfers between devices  11.9 us (15%)
  starting transfers between devices  10 us (12%)
  local copies, waits for them, and re-layouts  5.04 us (6%)
  other arithmetic  4.21 us (5%)
    pallas_call x3, Pallas kernels, exchange(): pl.pallas_call(exchange_kernel, out_shape=jax.ShapeDtypeStruct(values.sha...  18.1 us
    dot_general x1, matrix products, band_device(): jnp.einsum('ocn,onq->ocq', coef, legendre, preferred_element_type=jnp.flo...  14.4 us
    ppermute x6, waiting for transfers between devices, swap(): return lax.ppermute(values, 'freq', [(f, f ^ distance) for f in range(4)])  11.9 us
    ppermute x6, starting transfers between devices, swap(): return lax.ppermute(values, 'freq', [(f, f ^ distance) for f in range(4)])  10 us
    pallas_call x2, Pallas kernels, band_device(): pl.pallas_call(functools.partial(inverse_kernel, start), out_shape=(flat,...  6.14 us
    pallas_call x1, Pallas kernels, band_device(): pl.pallas_call(stokes_kernel, out_shape=jax.ShapeDtypeStruct((blocks, row...  5.63 us
    pallas_call x1, Pallas kernels, band_device(): pl.pallas_call(forward_kernel, out_shape=jax.ShapeDtypeStruct((blocks, ro...  4.04 us
  transfers between devices with their start and end apart: 6, of which 5 were waited for; matrix products, arithmetic and copies ran while one was open for 26% of the time, Pallas kernels for 6%

profile of v1, /device:TPU:0, one launch (start us, length us, event | category | flops | bytes accessed | tf_op | source)
XLA Modules:
  0.0 81.5 jit_solution(2404630669930003413)
XLA Ops:
  0.0 1.1 %convert_element_type.53 = f16[16,5400]{1,0:T(8,128)(2,1)S(1)} convert(f32[16,5400]{1,0:T(8,128)} %param.12) | non-fusion elementwise | flops 86400 | bytes 518400 | tf_op jit(solution)/shard_map/convert_element_type | solution.py:354
  1.1 4.1 %collective-permute-start = (f16[16,5400]{1,0:T(8,128)(2,1)S(1)}, f16[16,5400]{1,0:T(8,128)(2,1)S(1)}, u32[]{:S(2)}, u32[]{:S(2)}) collective-permute-start(f16[16,5400]{1,0:T(8,128)(2,1)S(1)} %convert_element_type.53), channel_id=1, source_target_pairs={{0,2},{1,3},{2,0},{3,1},{4,6},{5,7},{6,4},{7,5},{8,10},{9,11},{10,... | collective-permute-start | bytes 518408 | tf_op jit(solution)/shard_map/ppermute | solution.py:337
  5.2 0.8 reshape.25
  6.1 14.4 %convolution_convert_fusion = bf16[68,2,128]{2,1,0:T(2,128)(2,1)S(1)} fusion(bf16[68,2,2176]{2,1,0:T(2,128)(2,1)S(1)} %copy-done, bf16[68,2176,128]{2,1,0:T(8,128)(2,1)} %param.14), kind=kOutput, calls=%fused_computation.5 | convolution fusion | flops 75777024 | bytes 38506496 | tf_op jit(solution)/shard_map/ocn,onq->ocq/dot_general | solution.py:362
  20.8 5.0 %route_synth.1 = bf16[8,32,128]{2,1,0:T(8,128)(2,1)S(1)} custom-call(bf16[8,32,128]{2,1,0:T(8,128)(2,1)S(1)} %pad.18.src), custom_call_target="tpu_custom_call" | custom-call | tf_op jit(solution)/shard_map/route_synth/pallas_call | solution.py:319
  25.8 1.6 %fusion.2 = f32[32,1024]{1,0:T(8,128)} fusion(bf16[8,32,128]{2,1,0:T(8,128)(2,1)S(1)} %route_synth.1, s32[8,128]{1,0:T(8,128)S(1)} %pad.19), kind=kOutput, calls=%fused_computation.4 | convolution fusion | flops 68157440 | bytes 200704 | tf_op jit(solution)/shard_map/brs,bst->rt/dot_general | solution.py:371
  28.2 1.6 %collective-permute-start.1 = (f16[16,5400]{1,0:T(8,128)(2,1)}, f16[16,5400]{1,0:T(8,128)(2,1)}, u32[]{:S(2)}, u32[]{:S(2)}) collective-permute-start(f16[16,5400]{1,0:T(8,128)(2,1)} %select_convert_fusion), channel_id=1, source_target_pairs={{0,1},{1,0},{2,3},{3,2},{4,5},{5,4},{6,7},{7,6},{8,9},{9,8},{10,11... | collective-permute-start | bytes 518408 | tf_op jit(solution)/shard_map/ppermute | solution.py:337
  29.9 1.0 %reshape.26 = f32[16,2,16,64]{3,2,1,0:T(8,128)S(1)} reshape(f32[32,1024]{1,0:T(8,128)} %fusion.2) | data formatting | bytes 262144 | tf_op jit(solution)/shard_map/reshape | solution.py:372
  31.3 1.2 %copy.16 = bf16[255,8,45]{2,1,0:T(8,128)(2,1)} copy(bf16[255,8,45]{0,2,1:T(8,128)(2,1)S(1)} %reshape.22) | data formatting | bytes 367200 | tf_op jit(solution)/shard_map/reshape | solution.py:392
  32.5 1.2 %pad.17 = bf16[255,8,64]{2,1,0:T(8,128)(2,1)S(1)} pad(bf16[255,8,45]{2,1,0:T(8,128)(2,1)} %copy.16, bf16[]{:T(256)} %constant.82.clone.1), padding=0_0x0_0x0_19 | pad | bytes 444722 | tf_op jit(solution)/shard_map/jit(_pad)/pad | solution.py:393
  34.0 1.0 %collective-permute-done.1 = f16[16,5400]{1,0:T(8,128)(2,1)} collective-permute-done((f16[16,5400]{1,0:T(8,128)(2,1)}, f16[16,5400]{1,0:T(8,128)(2,1)}, u32[]{:S(2)}, u32[]{:S(2)}) %collective-permute-start.1) | collective-permute-done | bytes 172832 | tf_op jit(solution)/shard_map/ppermute | solution.py:337
  35.0 1.1 %fusion.5 = (f32[16,5400]{1,0:T(8,128)S(1)}, f32[16,5400]{1,0:T(8,128)S(1)}) fusion(f32[16,5400]{1,0:T(8,128)S(1)} %copy-done.7, f16[16,5400]{1,0:T(8,128)(2,1)S(1)} %collective-permute-done, pred[]{:T(512)S(6)} %lt.22, pred[]{:T(512)S(6)} %eq.28, f16[16,5400]{1,0:T(8,128)(2,1)} %collective-permute-done.1), kind=kLoop, calls=%fused_computation.15 | loop fusion | flops 1123200 | bytes 1382402 | tf_op jit(solution)/shard_map/jit(_where)/select_n | solution.py:360
  36.2 4.0 %longitude_forward.1.src = bf16[8,128,128]{2,1,0:T(8,128)(2,1)S(1)} custom-call(f32[16,5400]{1,0:T(8,128)S(1)} %get-tuple-element.14.re_ref, f32[16,5400]{1,0:T(8,128)S(1)} %get-tuple-element.13.im_ref, f32[16,16,128]{2,1,0:T(8,128)S(1)} %reshape.27.model_ref, f32[16,1,128]{2,1,0:T(1,128)S(1)} %broadcast_in_dim.7.weight_ref, ...), custom_call_target="tpu_custom_call" | custom-call | tf_op jit(solution)/shard_map/longitude_forward/pallas_call | solution.py:376
  40.2 6.6 %send_columns.1.weighted_ref = bf16[8,128,128]{2,1,0:T(8,128)(2,1)S(1)} custom-call(bf16[8,128,128]{2,1,0:T(8,128)(2,1)S(1)} %longitude_forward.1.src), custom_call_target="tpu_custom_call" | custom-call | tf_op jit(solution)/shard_map/send_columns/pallas_call | solution.py:319
  46.8 5.6 %stokes_rows.1.src = bf16[8,128,128]{2,1,0:T(8,128)(2,1)S(1)} custom-call(f32[255,8,128]{2,1,0:T(8,128)S(1)} %maximum_convert_fusion.kernel_ref, bf16[8,128,128]{2,1,0:T(8,128)(2,1)S(1)} %send_columns.1.weighted_ref), custom_call_target="tpu_custom_call" | custom-call | tf_op jit(solution)/shard_map/stokes_rows/pallas_call | solution.py:395
  52.5 6.5 %return_sums.1.in_ref = bf16[8,128,128]{2,1,0:T(8,128)(2,1)S(1)} custom-call(bf16[8,128,128]{2,1,0:T(8,128)(2,1)S(1)} %stokes_rows.1.src), custom_call_target="tpu_custom_call" | custom-call | tf_op jit(solution)/shard_map/return_sums/pallas_call | solution.py:319
  59.1 3.1 %longitude_inverse.3 = (f32[8,5400]{1,0:T(8,128)S(1)}, f32[8,5400]{1,0:T(8,128)S(1)}) custom-call(bf16[8,128,128]{2,1,0:T(8,128)(2,1)S(1)} %return_sums.1.in_ref, bf16[4,96,384]{2,1,0:T(8,128)(2,1)S(1)} %copy-done.2, f32[4,2,128,128]{3,2,1,0:T(8,128)S(1)} %copy-done.1, bf16[256,128]{1,0:T(8,128)(2,1)S(1)} %copy-done.5), custom_call_target="tpu_custom_call" | custom-call | tf_op jit(solution)/shard_map/longitude_inverse/pallas_call | solution.py:418
  62.1 3.1 %longitude_inverse.2 = (f32[8,5400]{1,0:T(8,128)S(1)}, f32[8,5400]{1,0:T(8,128)S(1)}) custom-call(bf16[8,128,128]{2,1,0:T(8,128)(2,1)S(1)} %return_sums.1.in_ref, bf16[4,96,384]{2,1,0:T(8,128)(2,1)S(1)} %copy-done.2, f32[4,2,128,128]{3,2,1,0:T(8,128)S(1)} %copy-done.1, bf16[256,128]{1,0:T(8,128)(2,1)S(1)} %copy-done.5), custom_call_target="tpu_custom_call" | custom-call | tf_op jit(solution)/shard_map/longitude_inverse/pallas_call | solution.py:418
  65.2 1.6 %collective-permute-start.2 = (f16[8,5400]{1,0:T(8,128)(2,1)S(1)}, f16[8,5400]{1,0:T(8,128)(2,1)S(1)}, u32[]{:S(2)}, u32[]{:S(2)}) collective-permute-start(f16[8,5400]{1,0:T(8,128)(2,1)S(1)} %multiply_convert_fusion.1), channel_id=1, source_target_pairs={{0,1},{1,0},{2,3},{3,2},{4,5},{5,4},{6,7},{7,6},{8,9},{9,8},{10,11... | collective-permute-start | bytes 259208 | tf_op jit(solution)/shard_map/ppermute | solution.py:337
  67.4 3.1 %collective-permute-done.2 = f16[8,5400]{1,0:T(8,128)(2,1)S(1)} collective-permute-done((f16[8,5400]{1,0:T(8,128)(2,1)S(1)}, f16[8,5400]{1,0:T(8,128)(2,1)S(1)}, u32[]{:S(2)}, u32[]{:S(2)}) %collective-permute-start.2) | collective-permute-done | bytes 86432 | tf_op jit(solution)/shard_map/ppermute | solution.py:337
  71.0 0.9 %collective-permute-done.4 = f16[8,5400]{1,0:T(8,128)(2,1)S(1)} collective-permute-done((f16[8,5400]{1,0:T(8,128)(2,1)S(1)}, f16[8,5400]{1,0:T(8,128)(2,1)S(1)}, u32[]{:S(2)}, u32[]{:S(2)}) %collective-permute-start.4) | collective-permute-done | bytes 86432 | tf_op jit(solution)/shard_map/ppermute | solution.py:337
  71.9 1.8 %collective-permute-start.5 = (f16[8,5400]{1,0:T(8,128)(2,1)S(1)}, f16[8,5400]{1,0:T(8,128)(2,1)S(1)}, u32[]{:S(2)}, u32[]{:S(2)}) collective-permute-start(f16[8,5400]{1,0:T(8,128)(2,1)S(1)} %fusion.15), channel_id=1, source_target_pairs={{0,2},{1,3},{2,0},{3,1},{4,6},{5,7},{6,4},{7,5},{8,10},{9,11},{10,... | collective-permute-start | bytes 259208 | tf_op jit(solution)/shard_map/ppermute | solution.py:337
  73.7 6.0 %collective-permute-done.3 = f16[8,5400]{1,0:T(8,128)(2,1)S(1)} collective-permute-done((f16[8,5400]{1,0:T(8,128)(2,1)S(1)}, f16[8,5400]{1,0:T(8,128)(2,1)S(1)}, u32[]{:S(2)}, u32[]{:S(2)}) %collective-permute-start.3) | collective-permute-done | bytes 86432 | tf_op jit(solution)/shard_map/ppermute | solution.py:337
  79.8 0.9 %collective-permute-done.5 = f16[8,5400]{1,0:T(8,128)(2,1)S(1)} collective-permute-done((f16[8,5400]{1,0:T(8,128)(2,1)S(1)}, f16[8,5400]{1,0:T(8,128)(2,1)S(1)}, u32[]{:S(2)}, u32[]{:S(2)}) %collective-permute-start.5) | collective-permute-done | bytes 86432 | tf_op jit(solution)/shard_map/ppermute | solution.py:337
  (44 shorter events, 3.8 us)
Async XLA Ops:
  0.0 6.0 %copy-start = (bf16[68,2,2176]{2,1,0:T(2,128)(2,1)S(1)}, bf16[68,2,2176]{2,1,0:T(2,128)(2,1)}, u32[]{:S(2)}) copy-start(bf16[68,2,2176]{2,1,0:T(2,128)(2,1)} %param.13) | copy-start | bytes 1775620
  1.1 26.4 %collective-permute-start = (f16[16,5400]{1,0:T(8,128)(2,1)S(1)}, f16[16,5400]{1,0:T(8,128)(2,1)S(1)}, u32[]{:S(2)}, u32[]{:S(2)}) collective-permute-start(f16[16,5400]{1,0:T(8,128)(2,1)S(1)} %convert_element_type.53), channel_id=1, source_target_pairs={{0,2},{1,3},{2,0},{3,1},{4,6},{5,7},{6,4},{7,5},{8,10},{9,11},{10,... | collective-permute-start | bytes 518408 | tf_op jit(solution)/shard_map/ppermute | solution.py:337
  6.0 14.5 %copy-start.9 = (s32[16]{0:T(128)S(1)}, s32[16]{0:T(128)}, u32[]{:S(2)}) copy-start(s32[16]{0:T(128)} %param.16) | copy-start | bytes 196
  6.1 21.4 %copy-start.7 = (f32[16,5400]{1,0:T(8,128)S(1)}, f32[16,5400]{1,0:T(8,128)}, u32[]{:S(2)}) copy-start(f32[16,5400]{1,0:T(8,128)} %param.12) | copy-start | bytes 1036804
  6.1 23.7 %copy-start.8 = (bf16[255,2700]{0,1:T(8,128)(2,1)S(1)}, bf16[255,2700]{0,1:T(8,128)(2,1)}, u32[]{:S(2)}) copy-start(bf16[255,2700]{0,1:T(8,128)(2,1)} %param.17) | copy-start | bytes 4131004
  28.2 8.0 %copy-start.3 = (bf16[4,128,288]{2,1,0:T(8,128)(2,1)S(1)}, bf16[4,128,288]{2,1,0:T(8,128)(2,1)}, u32[]{:S(2)}) copy-start(bf16[4,128,288]{2,1,0:T(8,128)(2,1)} %constant.98.clone.first_ref) | copy-start | bytes 884740
  28.2 8.0 %copy-start.4 = (f32[4,2,64,128]{3,2,1,0:T(8,128)S(1)}, f32[4,2,64,128]{3,2,1,0:T(8,128)}, u32[]{:S(2)}) copy-start(f32[4,2,64,128]{3,2,1,0:T(8,128)} %constant.99.clone.twist_ref) | copy-start | bytes 786436
  28.2 8.0 %copy-start.6 = (bf16[128,384]{1,0:T(8,128)(2,1)S(1)}, bf16[128,384]{1,0:T(8,128)(2,1)}, u32[]{:S(2)}) copy-start(bf16[128,384]{1,0:T(8,128)(2,1)} %constant.100.clone.second_ref) | copy-start | bytes 294916
  28.2 6.8 %collective-permute-start.1 = (f16[16,5400]{1,0:T(8,128)(2,1)}, f16[16,5400]{1,0:T(8,128)(2,1)}, u32[]{:S(2)}, u32[]{:S(2)}) collective-permute-start(f16[16,5400]{1,0:T(8,128)(2,1)} %select_convert_fusion), channel_id=1, source_target_pairs={{0,1},{1,0},{2,3},{3,2},{4,5},{5,4},{6,7},{7,6},{8,9},{9,8},{10,11... | collective-permute-start | bytes 518408 | tf_op jit(solution)/shard_map/ppermute | solution.py:337
  32.5 26.6 %copy-start.1 = (f32[4,2,128,128]{3,2,1,0:T(8,128)S(1)}, f32[4,2,128,128]{3,2,1,0:T(8,128)}, u32[]{:S(2)}) copy-start(f32[4,2,128,128]{3,2,1,0:T(8,128)} %constant.102.clone.twist_ref) | copy-start | bytes 1572868
  32.5 26.6 %copy-start.2 = (bf16[4,96,384]{2,1,0:T(8,128)(2,1)S(1)}, bf16[4,96,384]{2,1,0:T(8,128)(2,1)}, u32[]{:S(2)}) copy-start(bf16[4,96,384]{2,1,0:T(8,128)(2,1)} %constant.101.clone.first_ref) | copy-start | bytes 884740
  32.5 26.6 %copy-start.5 = (bf16[256,128]{1,0:T(8,128)(2,1)S(1)}, bf16[256,128]{1,0:T(8,128)(2,1)}, u32[]{:S(2)}) copy-start(bf16[256,128]{1,0:T(8,128)(2,1)} %constant.103.clone.second_ref) | copy-start | bytes 196612
  65.2 5.3 %collective-permute-start.2 = (f16[8,5400]{1,0:T(8,128)(2,1)S(1)}, f16[8,5400]{1,0:T(8,128)(2,1)S(1)}, u32[]{:S(2)}, u32[]{:S(2)}) collective-permute-start(f16[8,5400]{1,0:T(8,128)(2,1)S(1)} %multiply_convert_fusion.1), channel_id=1, source_target_pairs={{0,1},{1,0},{2,3},{3,2},{4,5},{5,4},{6,7},{7,6},{8,9},{9,8},{10,11... | collective-permute-start | bytes 259208 | tf_op jit(solution)/shard_map/ppermute | solution.py:337
  66.9 5.0 %collective-permute-start.4 = (f16[8,5400]{1,0:T(8,128)(2,1)S(1)}, f16[8,5400]{1,0:T(8,128)(2,1)S(1)}, u32[]{:S(2)}, u32[]{:S(2)}) collective-permute-start(f16[8,5400]{1,0:T(8,128)(2,1)S(1)} %multiply_convert_fusion), channel_id=1, source_target_pairs={{0,1},{1,0},{2,3},{3,2},{4,5},{5,4},{6,7},{7,6},{8,9},{9,8},{10,11... | collective-permute-start | bytes 259208 | tf_op jit(solution)/shard_map/ppermute | solution.py:337
  70.6 9.1 %collective-permute-start.3 = (f16[8,5400]{1,0:T(8,128)(2,1)S(1)}, f16[8,5400]{1,0:T(8,128)(2,1)S(1)}, u32[]{:S(2)}, u32[]{:S(2)}) collective-permute-start(f16[8,5400]{1,0:T(8,128)(2,1)S(1)} %fusion.10), channel_id=1, source_target_pairs={{0,2},{1,3},{2,0},{3,1},{4,6},{5,7},{6,4},{7,5},{8,10},{9,11},{10,... | collective-permute-start | bytes 259208 | tf_op jit(solution)/shard_map/ppermute | solution.py:337
  71.9 8.8 %collective-permute-start.5 = (f16[8,5400]{1,0:T(8,128)(2,1)S(1)}, f16[8,5400]{1,0:T(8,128)(2,1)S(1)}, u32[]{:S(2)}, u32[]{:S(2)}) collective-permute-start(f16[8,5400]{1,0:T(8,128)(2,1)S(1)} %fusion.15), channel_id=1, source_target_pairs={{0,2},{1,3},{2,0},{3,1},{4,6},{5,7},{6,4},{7,5},{8,10},{9,11},{10,... | collective-permute-start | bytes 259208 | tf_op jit(solution)/shard_map/ppermute | solution.py:337

commit v2 on v0

--- a/solution.py
+++ b/solution.py
@@ -134,7 +134,6 @@
 HALF = 64
 CP = 128
 SCALE = (2.0 / L) ** 0.5
-SHIFT = 2.0**-7
 
 
 def split_pair(values):
@@ -192,9 +191,87 @@
     return jnp.where(lane < HALF, 1.0, -1.0)
 
 
-def forward_kernel(re_ref, im_ref, model_ref, weight_ref, first_ref, twist_ref, second_ref, out_ref, grid):
+PIECES = ((0, 12), (12, 24), (24, 36), (36, 45))
+
+
+def start_remote(src, dst, send, recv, axis, peer):
+    copy = pltpu.make_async_remote_copy(
+        src_ref=src,
+        dst_ref=dst,
+        send_sem=send,
+        recv_sem=recv,
+        device_id={axis: peer},
+        device_id_type=pl.DeviceIdType.MESH,
+    )
+    copy.start()
+    return copy
+
+
+def residual_kernel(
+    re_ref,
+    im_ref,
+    synth_ref,
+    select_ref,
+    weight_ref,
+    kernel_ref,
+    first_ref,
+    twist_ref,
+    second_ref,
+    back_first_ref,
+    back_twist_ref,
+    back_second_ref,
+    out_ref,
+    grid,
+    parts,
+    routed,
+    model,
+    leaving,
+    columns,
+    values,
+    sums,
+    leaving_sums,
+    returned,
+    wire_one,
+    wire_two,
+    in_one,
+    in_two,
+    keep,
+    near,
+    route_send,
+    route_recv,
+    column_send,
+    column_recv,
+    sum_send,
+    sum_recv,
+    one_send,
+    one_recv,
+    two_send,
+    two_recv,
+):
+    me = lax.axis_index("lat")
     band = lax.axis_index("freq")
+    blocks = synth_ref.shape[0]
     rows = re_ref.shape[0]
+    deep = HALF // blocks
+    total = rows * blocks
+    held = model.shape[1]
+    peers = [lax.rem(me + d, blocks) for d in range(1, blocks)]
+    beside = band + 1 - 2 * lax.rem(band, 2)
+    across = lax.rem(band + 2, 4)
+    barrier = pltpu.get_barrier_semaphore()
+    for peer in peers:
+        pl.semaphore_signal(barrier, inc=1, device_id={"lat": peer}, device_id_type=pl.DeviceIdType.MESH)
+    for peer in (beside, across):
+        pl.semaphore_signal(barrier, inc=1, device_id={"freq": peer}, device_id_type=pl.DeviceIdType.MESH)
+    pl.semaphore_wait(barrier, blocks + 1)
+
+    routes = [
+        start_remote(synth_ref.at[peer], routed.at[me], route_send.at[d], route_recv.at[d], "lat", peer)
+        for d, peer in enumerate(peers)
+    ]
+    own = pltpu.make_async_copy(synth_ref.at[me], routed.at[me], near)
+    own.start()
+
     grid[...] = jnp.zeros_like(grid)
     for a in range(NA):
         grid[:, a, :NC] = re_ref[:, a * NC : (a + 1) * NC]
@@ -212,67 +289,119 @@
             second, cols_of_three(turned), (((1,), (1,)), ((), ())), preferred_element_type=jnp.float32
         )
         spectrum = both[:HALF] * SCALE + pltpu.roll(both[HALF:], HALF, 1) * sign
-        held = model_ref.shape[1]
-        weight = weight_ref[r]
-        out_ref[r, :held] = (spectrum[:held] - model_ref[r]) * weight
-        out_ref[r, held:] = spectrum[held:] * weight
-
-
-def inverse_kernel(in_ref, first_ref, twist_ref, second_ref, re_ref, own_ref, grid):
-    band = lax.axis_index("freq")
-    rows = in_ref.shape[0]
-    first = first_ref[band]
-    cosine = twist_ref[band, 0]
-    sine = twist_ref[band, 1]
-    second = second_ref[...]
-    sign = lane_sign() * SCALE
+        parts[:, r * deep : (r + 1) * deep] = spectrum.reshape(blocks, deep, CP)
+
+    own.wait()
+    for copy in routes:
+        copy.wait()
+    found = jnp.zeros((2 * rows, held * HALF), jnp.float32)
+    for source in range(blocks):
+        found = found + jnp.dot(routed[source], select_ref[source], preferred_element_type=jnp.float32)
+    for j in range(held):
+        span = slice(j * HALF, (j + 1) * HALF)
+        model[:, j] = jnp.concatenate([found[:rows, span], found[rows:, span]], axis=1)
     for r in range(rows):
-        both = jnp.dot(second, rows_of_three(in_ref[r]), preferred_element_type=jnp.float32)
-        middle = both[:CP] * SCALE - pltpu.roll(both[CP:], HALF, 1) * sign
-        turned = middle * cosine + pltpu.roll(middle, HALF, 1) * sine
-        grid[r] = lax.dot_general(
-            first, cols_of_three(turned), (((1,), (1,)), ((), ())), preferred_element_type=jnp.float32
-        )
-    even = band % 2 == 0
-    for a in range(NA):
-        real = grid[:, a, :NC]
-        re_ref[:, a * NC : (a + 1) * NC] = real
-        own_ref[:, a * NC : (a + 1) * NC] = jnp.where(even, real, grid[:, AP + a, :NC])
-
-
-def stokes_kernel(kernel_ref, weighted_ref, out_ref):
-    total = weighted_ref.shape[0]
-    pb, qb = 16, 8
-
-    def p_step(i, carry):
-        p0 = i * pb
+        span = slice(r * deep, (r + 1) * deep)
+        taken = model[r]
+        for k in range(blocks):
+            term = parts[k, span]
+            if k * deep < held:
+                term = term - taken[k * deep : (k + 1) * deep]
+            parts[k, span] = term * weight_ref[r]
+    leaving[...] = parts[...].astype(leaving.dtype)
+
+    sent = [
+        start_remote(leaving.at[peer], columns.at[me], column_send.at[d], column_recv.at[d], "lat", peer)
+        for d, peer in enumerate(peers)
+    ]
+    own = pltpu.make_async_copy(leaving.at[me], columns.at[me], near)
+    own.start()
+    own.wait()
+    for copy in sent:
+        copy.wait()
+    for source in range(blocks):
+        values[source * rows : (source + 1) * rows] = columns[source].astype(jnp.float32).reshape(rows, deep, CP)
+
+    qb = 8
+    backs = []
+    for d, peer in enumerate(peers + [me]):
+        p0 = peer * rows
 
         def q_step(j, acc):
             q0 = j * qb
-            base = q0 - p0 + total - 1 - (pb - 1)
-            window = [kernel_ref[base + d] for d in range(pb + qb - 1)]
-            values = [weighted_ref[q0 + q].astype(jnp.float32) for q in range(qb)]
+            base = q0 - p0 + total - rows
+            window = [kernel_ref[base + e] for e in range(rows + qb - 1)]
+            terms = [values[q0 + q] for q in range(qb)]
             acc = list(acc)
-            for p in range(pb):
+            for p in range(rows):
                 for q in range(qb):
-                    acc[p] = acc[p] + window[q - p + pb - 1] * values[q]
+                    acc[p] = acc[p] + window[q - p + rows - 1] * terms[q]
             return tuple(acc)
 
-        zero = jnp.zeros(out_ref.shape[1:], jnp.float32)
-        acc = lax.fori_loop(0, total // qb, q_step, (zero,) * pb)
-        for p in range(pb):
-            out_ref[p0 + p] = acc[p]
-        return carry
-
-    lax.fori_loop(0, total // pb, p_step, 0)
+        zero = jnp.zeros((deep, CP), jnp.float32)
+        acc = lax.fori_loop(0, total // qb, q_step, (zero,) * rows)
+        for p in range(rows):
+            sums[p] = acc[p]
+        block = sums[...].reshape(rows * deep, CP).astype(leaving_sums.dtype)
+        if d < blocks - 1:
+            leaving_sums[d] = block
+            backs.append(
+                start_remote(leaving_sums.at[d], returned.at[me], sum_send.at[d], sum_recv.at[d], "lat", peer)
+            )
+        else:
+            returned[me] = block
+    for copy in backs:
+        copy.wait()
+
+    back_first = back_first_ref[band]
+    back_cosine = back_twist_ref[band, 0]
+    back_sine = back_twist_ref[band, 1]
+    back_second = back_second_ref[...]
+    parts[...] = returned[...].astype(jnp.float32)
+    for r in range(rows):
+        held_sums = parts[:, r * deep : (r + 1) * deep].reshape(HALF, CP).astype(jnp.bfloat16)
+        both = jnp.dot(
+            back_second, jnp.concatenate([held_sums, held_sums], axis=0), preferred_element_type=jnp.float32
+        )
+        middle = both[:CP] * SCALE - pltpu.roll(both[CP:], HALF, 1) * sign
+        turned = middle * back_cosine + pltpu.roll(middle, HALF, 1) * back_sine
+        grid[r] = lax.dot_general(
+            back_first, cols_of_three(turned), (((1,), (1,)), ((), ())), preferred_element_type=jnp.float32
+        )
+
+    even = 1.0 - lax.rem(band, 2).astype(jnp.float32)
+    keep_own = jnp.where((band == 1) | (band == 3), -1.0, 1.0)
+    keep_beside = jnp.where(band < 2, 1.0, -1.0)
+    give_beside = jnp.where((band == 1) | (band == 2), 1.0, -1.0)
+    ones = []
+    for k, (low, high) in enumerate(PIECES):
+        for a in range(low, high):
+            real = grid[:, a]
+            wire_one[a] = real.astype(wire_one.dtype)
+            keep[a] = even * real + (1.0 - even) * grid[:, AP + a]
+        piece = pl.ds(low, high - low)
+        ones.append(
+            start_remote(wire_one.at[piece], in_one.at[piece], one_send.at[k], one_recv.at[k], "freq", beside)
+        )
+    twos = []
+    for k, (low, high) in enumerate(PIECES):
+        ones[k].wait()
+        piece = pl.ds(low, high - low)
+        chosen = keep[low:high]
+        arrived = in_one[low:high].astype(jnp.float32)
+        wire_two[low:high] = (chosen + give_beside * arrived).astype(wire_two.dtype)
+        keep[low:high] = keep_own * chosen + keep_beside * arrived
+        twos.append(
+            start_remote(wire_two.at[piece], in_two.at[piece], two_send.at[k], two_recv.at[k], "freq", across)
+        )
+    for k, (low, high) in enumerate(PIECES):
+        twos[k].wait()
+        for a in range(low, high):
+            out_ref[:, a * NC : (a + 1) * NC] = (keep[a] + in_two[a].astype(jnp.float32))[:, :NC]
 
 
 def swap(values, distance):
     return lax.ppermute(values, "freq", [(f, f ^ distance) for f in range(4)])
-
-
-def pick(values, band):
-    return jnp.asarray(values, jnp.float32)[band]
 
 
 def band_device(gravity, coef, legendre, order_table, band_rows, kernel):
@@ -285,7 +414,6 @@
     deep = HALF // blocks
     first, twist, second = tables()
     vmem = pl.BlockSpec(memory_space=pltpu.VMEM)
-    params = pltpu.CompilerParams(vmem_limit_bytes=48 * 2**20)
 
     even = band % 2 == 0
     lower = band < 2
@@ -298,64 +426,84 @@
     h_im = jnp.where(even, 0.0, jnp.where(lower, -taken, taken))
 
     synth = jnp.einsum("ocn,onq->ocq", coef, legendre, preferred_element_type=jnp.float32).astype(jnp.bfloat16)
-    routed = lax.all_to_all(synth, "lat", split_axis=2, concat_axis=0, tiled=True)
+    synth = synth.reshape(slots, 2, blocks, rows).transpose(2, 1, 3, 0).reshape(blocks, 2 * rows, slots)
+    synth = jnp.pad(synth, ((0, 0), (0, 0), (0, CP - slots)))
     held = -(-(-(-order_table.shape[0] // 4) // NA) // 8) * 8
     mine = lax.dynamic_index_in_dim(order_table.reshape(blocks, 4, slots), band, 1, keepdims=False)
-    place = mine.reshape(-1) // 4
-    lane = place // NA * HALF + place % NA
-    selector = (lane[:, None] == jnp.arange(held * HALF, dtype=jnp.int32)[None, :]).astype(jnp.bfloat16)
-    model = jnp.einsum("jcr,jt->rct", routed, selector, preferred_element_type=jnp.float32)
-    model = model.reshape(rows, 2, held, HALF).transpose(0, 2, 1, 3).reshape(rows, held, 2 * HALF)
+    place = mine // 4
+    lane = jnp.pad(place // NA * HALF + place % NA, ((0, 0), (0, CP - slots)), constant_values=-1)
+    selector = (lane[:, :, None] == jnp.arange(held * HALF, dtype=jnp.int32)).astype(jnp.bfloat16)
     weight = jnp.cos((20.0 + band_rows.astype(jnp.float32) / 60.0) * (np.pi / 180.0))
     weight = jnp.broadcast_to(weight[:, None, None], (rows, 1, CP))
-
-    forward_twist = twist.astype(np.float32)
-    weighted = pl.pallas_call(
-        forward_kernel,
-        out_shape=jax.ShapeDtypeStruct((rows, HALF, CP), jnp.float32),
-        in_specs=[vmem] * 7,
-        out_specs=vmem,
-        scratch_shapes=[pltpu.VMEM((rows, 2 * AP, CP), jnp.float32)],
-        compiler_params=params,
-        name="longitude_forward",
-    )(h_re, h_im, model, weight, three_cols(first), forward_twist, three_cols(second))
-    weighted = weighted.astype(jnp.bfloat16).reshape(rows, blocks, deep, CP)
-    columns = lax.all_to_all(weighted, "lat", split_axis=1, concat_axis=0, tiled=True).reshape(total, deep, CP)
 
     width = deep * NA
     padded = jnp.pad(kernel, ((0, 0), (0, width * blocks - kernel.shape[1])))
     own = lax.dynamic_slice_in_dim(padded, block * width, width, 1).reshape(2 * total - 1, deep, NA)
     own = jnp.pad(own, ((0, 0), (0, 0), (0, HALF - NA)))
     own = jnp.concatenate([own, own], axis=2).astype(jnp.float32)
-    summed = pl.pallas_call(
-        stokes_kernel,
-        out_shape=jax.ShapeDtypeStruct((total, deep, CP), jnp.float32),
-        in_specs=[vmem] * 2,
-        out_specs=vmem,
-        compiler_params=params,
-        name="stokes_rows",
-    )(own, columns)
-    returned = lax.all_to_all(summed.reshape(total, 1, deep, CP), "lat", split_axis=0, concat_axis=1, tiled=True)
-
-    back_second = three_cols(np.concatenate([second[:HALF].T, second[HALF:].T], axis=0))
+
+    back_second = np.concatenate([second[:HALF].T, second[HALF:].T], axis=0)
+    back_second = np.concatenate(numpy_pair(back_second), axis=1)
     turn = np.concatenate([twist[:, 0], twist[:, 0]], axis=1), np.concatenate([-twist[:, 1], twist[:, 1]], axis=1)
     back_twist = np.stack([turn[0].transpose(0, 2, 1), turn[1].transpose(0, 2, 1)], axis=1).astype(np.float32)
     back_first = three_cols(first.transpose(0, 2, 1))
-    flat = jax.ShapeDtypeStruct(gravity.shape, jnp.float32)
-    real, chosen = pl.pallas_call(
-        inverse_kernel,
-        out_shape=(flat, flat),
-        in_specs=[vmem] * 4,
-        out_specs=(vmem, vmem),
-        scratch_shapes=[pltpu.VMEM((rows, 2 * AP, CP), jnp.float32)],
-        compiler_params=params,
-        name="longitude_inverse",
-    )(returned.reshape(rows, HALF, CP), back_first, back_twist, back_second)
-
-    beside = swap((real * SHIFT).astype(jnp.float16), 1).astype(jnp.float32) / SHIFT
-    keep = pick([1, -1, 1, -1], band) * chosen + pick([1, 1, -1, -1], band) * beside
-    give = chosen + pick([-1, 1, 1, -1], band) * beside
-    return keep + swap((give * SHIFT).astype(jnp.float16), 2).astype(jnp.float32) / SHIFT
+
+    lanes = (blocks, rows * deep, CP)
+    line = (NA, rows, CP)
+    wire = jnp.bfloat16
+    peers = pltpu.SemaphoreType.DMA((blocks - 1,))
+    pieces = pltpu.SemaphoreType.DMA((len(PIECES),))
+    return pl.pallas_call(
+        residual_kernel,
+        out_shape=jax.ShapeDtypeStruct(gravity.shape, jnp.float32),
+        in_specs=[vmem] * 12,
+        out_specs=vmem,
+        scratch_shapes=[
+            pltpu.VMEM((rows, 2 * AP, CP), jnp.float32),
+            pltpu.VMEM(lanes, jnp.float32),
+            pltpu.VMEM(synth.shape, jnp.bfloat16),
+            pltpu.VMEM((rows, held, CP), jnp.float32),
+            pltpu.VMEM(lanes, wire),
+            pltpu.VMEM(lanes, wire),
+            pltpu.VMEM((total, deep, CP), jnp.float32),
+            pltpu.VMEM((rows, deep, CP), jnp.float32),
+            pltpu.VMEM((blocks - 1, rows * deep, CP), wire),
+            pltpu.VMEM(lanes, wire),
+            pltpu.VMEM(line, wire),
+            pltpu.VMEM(line, wire),
+            pltpu.VMEM(line, wire),
+            pltpu.VMEM(line, wire),
+            pltpu.VMEM(line, jnp.float32),
+            pltpu.SemaphoreType.DMA,
+            peers,
+            peers,
+            peers,
+            peers,
+            peers,
+            peers,
+            pieces,
+            pieces,
+            pieces,
+            pieces,
+        ],
+        compiler_params=pltpu.CompilerParams(
+            collective_id=0, has_side_effects=True, vmem_limit_bytes=48 * 2**20
+        ),
+        name="residual_band",
+    )(
+        h_re,
+        h_im,
+        synth,
+        selector,
+        weight,
+        own,
+        three_cols(first),
+        twist.astype(np.float32),
+        three_cols(second),
+        back_first,
+        back_twist,
+        back_second,
+    )
 
 
 def fits(mesh):

time: 87.6 us -> 74.4 us (0.85)
  Pallas kernels: 11.8 us -> 37.9 us
  waiting for transfers between devices: 23.8 us -> 0.01 us
  blocking collectives: 12.3 us -> 0 us
  starting transfers between devices: 14.9 us -> 5.61 us
  local copies, waits for them, and re-layouts: 5 us -> 10.5 us
  other arithmetic: 3.24 us -> 5.47 us
  between operations: 1.67 us -> 0.2 us
    pallas_call x3 -> x1, Pallas kernels: 11.8 us -> 37.9 us  [band_device(): pl.pallas_call(residual_kernel, out_shape=jax.ShapeDtypeStruct(gravity.sh...]
    ppermute x4 -> x2, waiting for transfers between devices: 13.2 us -> 0.01 us  [swap(): return lax.ppermute(values, 'freq', [(f, f ^ distance) for f in range(4)])]
    all_to_all x1 -> x0, blocking collectives: 12.3 us -> none  [band_device(): lax.all_to_all(summed.reshape(total, 1, deep, CP), 'lat', split_axis=0, c...]
    all_to_all x2 -> x0, waiting for transfers between devices: 10.5 us -> none  [the longest x1 5.87 us: band_device(): lax.all_to_all(weighted, 'lat', split_axis=1, concat_axis=0, tiled=True)]
    all_to_all x2 -> x0, starting transfers between devices: 7.14 us -> none  [the longest x1 3.72 us: band_device(): lax.all_to_all(synth, 'lat', split_axis=2, concat_axis=0, tiled=True)]
    reshape x2, local copies, waits for them, and re-layouts: 0.43 us -> 3.73 us  [band_device(): lax.dynamic_slice_in_dim(padded, block * width, width, 1)]
    ppermute x4 -> x2, starting transfers between devices: 7.8 us -> 5.61 us  [swap(): return lax.ppermute(values, 'freq', [(f, f ^ distance) for f in range(4)])]
    dynamic_slice x3 -> x0, local copies, waits for them, and re-layouts: 1.79 us -> none  [pick(): return jnp.asarray(values, jnp.float32)[band]]
  transfers between devices with their start and end apart: 6 -> 2, of which waited for: 5 -> 0; matrix products, arithmetic and copies ran while one was open for 22% -> 33% of each run, Pallas kernels for 0% -> 0%
where the time goes in v2:
time: 74.4 us; the launch traced here: 74 us
  Pallas kernels  37.9 us (51%)
  matrix products  14.4 us (19%)
  local copies, waits for them, and re-layouts  10.5 us (14%)
  starting transfers between devices  5.61 us (8%)
  other arithmetic  5.47 us (7%)
    pallas_call x1, Pallas kernels, band_device(): pl.pallas_call(residual_kernel, out_shape=jax.ShapeDtypeStruct(gravity.sh...  37.9 us
    dot_general x1, matrix products, band_device(): jnp.einsum('ocn,onq->ocq', coef, legendre, preferred_element_type=jnp.flo...  14.4 us
    ppermute x2, starting transfers between devices, swap(): return lax.ppermute(values, 'freq', [(f, f ^ distance) for f in range(4)])  5.61 us
    reshape x2, local copies, waits for them, and re-layouts, band_device(): lax.dynamic_slice_in_dim(padded, block * width, width, 1)  3.73 us
    convert_element_type x1, other arithmetic, band_device(): short = gravity.astype(jnp.float16)  1.73 us
    convert_element_type x1, other arithmetic, band_device(): jnp.where(even, taken, added).astype(jnp.float16)  1.73 us
  transfers between devices with their start and end apart: 2, of which 0 were waited for; matrix products, arithmetic and copies ran while one was open for 33% of the time, Pallas kernels for 0%

profile of v2, /device:TPU:0, one launch (start us, length us, event | category | flops | bytes accessed | tf_op | source)
XLA Modules:
  0.0 74.0 jit_solution(128983028460115043)
XLA Ops:
  0.0 1.7 %convert_element_type.30 = f16[16,5400]{1,0:T(8,128)(2,1)} convert(f32[16,5400]{1,0:T(8,128)} %param.12) | non-fusion elementwise | flops 86400 | bytes 518400 | tf_op jit(solution)/shard_map/convert_element_type | solution.py:420
  1.7 4.0 %collective-permute-start = (f16[16,5400]{1,0:T(8,128)(2,1)}, f16[16,5400]{1,0:T(8,128)(2,1)}, u32[]{:S(2)}, u32[]{:S(2)}) collective-permute-start(f16[16,5400]{1,0:T(8,128)(2,1)} %convert_element_type.30), channel_id=1, source_target_pairs={{0,2},{1,3},{2,0},{3,1},{4,6},{5,7},{6,4},{7,5},{8,10},{9,11},{10,... | collective-permute-start | bytes 518408 | tf_op jit(solution)/shard_map/ppermute | solution.py:404
  5.8 0.8 %reshape.18 = s32[8,4,68]{2,1,0:T(4,128)S(1)} reshape(s32[2176]{0:T(1024)} %param.15) | data formatting | bytes 17408 | tf_op jit(solution)/shard_map/reshape | solution.py:432
  6.6 0.4 fusion.select_ref
  7.1 0.0 copy-start.9
  7.1 0.0 copy-start.7
  7.1 0.0 copy-start.8
  7.1 14.4 %convolution_convert_fusion = bf16[68,2,128]{2,1,0:T(2,128)(2,1)S(1)} fusion(bf16[68,2,2176]{2,1,0:T(2,128)(2,1)S(1)} %copy-done, bf16[68,2176,128]{2,1,0:T(8,128)(2,1)} %param.14), kind=kOutput, calls=%fused_computation.3 | convolution fusion | flops 75777024 | bytes 38506496 | tf_op jit(solution)/shard_map/ocn,onq->ocq/dot_general | solution.py:428
  21.5 0.0 copy-start.1
  21.6 0.0 copy-start.3
  21.6 1.7 %select_convert_fusion = f16[16,5400]{1,0:T(8,128)(2,1)} fusion(f32[16,5400]{1,0:T(8,128)S(1)} %copy-done.7, f16[16,5400]{1,0:T(8,128)(2,1)} %collective-permute-done, pred[]{:T(512)S(6)} %lt.21, pred[]{:T(512)S(6)} %eq.20), kind=kLoop, calls=%fused_computation.14 | loop fusion | flops 604800 | bytes 691202 | tf_op jit(solution)/shard_map/convert_element_type | solution.py:424
  23.4 1.6 %collective-permute-start.1 = (f16[16,5400]{1,0:T(8,128)(2,1)}, f16[16,5400]{1,0:T(8,128)(2,1)}, u32[]{:S(2)}, u32[]{:S(2)}) collective-permute-start(f16[16,5400]{1,0:T(8,128)(2,1)} %select_convert_fusion), channel_id=1, source_target_pairs={{0,1},{1,0},{2,3},{3,2},{4,5},{5,4},{6,7},{7,6},{8,9},{9,8},{10,11... | collective-permute-start | bytes 518408 | tf_op jit(solution)/shard_map/ppermute | solution.py:404
  24.9 0.8 %pad_dynamic-slice_fusion = bf16[255,360]{0,1:T(8,128)(2,1)} fusion(s32[]{:T(128)S(6)} %select_n.73, bf16[255,2700]{0,1:T(8,128)(2,1)S(1)} %copy-done.8), kind=kLoop, calls=%fused_computation.2 | loop fusion | bytes 1560604 | tf_op jit(solution)/shard_map/dynamic_slice | solution.py:441
  25.7 0.7 %copy.15 = bf16[68,2,128]{0,2,1:T(8,128)(2,1)} copy(bf16[68,2,128]{2,1,0:T(2,128)(2,1)S(1)} %convolution_convert_fusion) | data formatting | bytes 69632 | tf_op jit(solution)/shard_map/convert_element_type | solution.py:428
  26.5 1.5 %copy.16 = bf16[8,2,16,68]{3,2,1,0:T(8,128)(2,1)} copy(bf16[8,2,16,68]{3,2,0,1:T(8,128)(2,1)} %bitcast.10) | data formatting | bytes 69632 | tf_op jit(solution)/shard_map/transpose | solution.py:429
  27.9 1.7 %reshape.19 = bf16[255,8,45]{0,2,1:T(8,128)(2,1)} reshape(bf16[255,360]{0,1:T(8,128)(2,1)} %pad_dynamic-slice_fusion) | data formatting | bytes 367200 | tf_op jit(solution)/shard_map/reshape | solution.py:441
  29.6 2.1 %copy.17 = bf16[255,8,45]{2,1,0:T(8,128)(2,1)} copy(bf16[255,8,45]{0,2,1:T(8,128)(2,1)} %reshape.19) | data formatting | bytes 367200 | tf_op jit(solution)/shard_map/reshape | solution.py:441
  31.6 0.9 %pad.16.synth_ref = bf16[8,32,128]{2,1,0:T(8,128)(2,1)S(1)} pad(bf16[8,32,68]{2,1,0:T(8,128)(2,1)} %bitcast.9, bf16[]{:T(256)} %constant.73.clone.1), padding=0_0x0_0x0_60 | pad | bytes 100354 | tf_op jit(solution)/shard_map/jit(_pad)/pad | solution.py:430
  32.6 1.1 %pad.19 = bf16[255,8,64]{2,1,0:T(8,128)(2,1)S(1)} pad(bf16[255,8,45]{2,1,0:T(8,128)(2,1)} %copy.17, bf16[]{:T(256)} %constant.73.clone.1), padding=0_0x0_0x0_19 | pad | bytes 444722 | tf_op jit(solution)/shard_map/jit(_pad)/pad | solution.py:442
  33.7 0.3 maximum_convert_fusion.kernel_ref
  34.0 1.3 %fusion.3 = (f32[16,5400]{1,0:T(8,128)S(1)}, f32[16,5400]{1,0:T(8,128)S(1)}) fusion(f32[16,5400]{1,0:T(8,128)} %param.12, f16[16,5400]{1,0:T(8,128)(2,1)} %collective-permute-done, pred[]{:T(512)S(6)} %lt.21, pred[]{:T(512)S(6)} %eq.20, f16[16,5400]{1,0:T(8,128)(2,1)} %collective-permute-done.1), kind=kLoop, calls=%fused_computation.13 | loop fusion | flops 1123200 | bytes 1382402 | tf_op jit(solution)/shard_map/jit(_where)/select_n | solution.py:426
  35.3 0.1 broadcast_in_dim.7.weight_ref
  35.4 37.9 %residual_band.1 = f32[16,5400]{1,0:T(8,128)S(1)} custom-call(f32[16,5400]{1,0:T(8,128)S(1)} %get-tuple-element.6.re_ref, f32[16,5400]{1,0:T(8,128)S(1)} %get-tuple-element.5.im_ref, bf16[8,32,128]{2,1,0:T(8,128)(2,1)S(1)} %pad.16.synth_ref, bf16[8,128,1024]{2,1,0:T(8,128)(2,1)S(1)} %fusion.select_ref, f32[16,1,128]{2,1,0:T(1,128)S(1)} %broadcast_in_dim.7.weight_ref, ...), custom_call_target="tpu_custom_call" | custom-call | tf_op jit(solution)/shard_map/residual_band/pallas_call | solution.py:456
  73.3 0.7 copy.19
  (21 shorter events, 0.1 us)
Async XLA Ops:
  0.0 7.1 %copy-start = (bf16[68,2,2176]{2,1,0:T(2,128)(2,1)S(1)}, bf16[68,2,2176]{2,1,0:T(2,128)(2,1)}, u32[]{:S(2)}) copy-start(bf16[68,2,2176]{2,1,0:T(2,128)(2,1)} %param.13) | copy-start | bytes 1775620
  1.7 19.9 %collective-permute-start = (f16[16,5400]{1,0:T(8,128)(2,1)}, f16[16,5400]{1,0:T(8,128)(2,1)}, u32[]{:S(2)}, u32[]{:S(2)}) collective-permute-start(f16[16,5400]{1,0:T(8,128)(2,1)} %convert_element_type.30), channel_id=1, source_target_pairs={{0,2},{1,3},{2,0},{3,1},{4,6},{5,7},{6,4},{7,5},{8,10},{9,11},{10,... | collective-permute-start | bytes 518408 | tf_op jit(solution)/shard_map/ppermute | solution.py:404
  7.1 14.5 %copy-start.9 = (s32[16]{0:T(128)S(1)}, s32[16]{0:T(128)}, u32[]{:S(2)}) copy-start(s32[16]{0:T(128)} %param.16) | copy-start | bytes 196
  7.1 14.5 %copy-start.7 = (f32[16,5400]{1,0:T(8,128)S(1)}, f32[16,5400]{1,0:T(8,128)}, u32[]{:S(2)}) copy-start(f32[16,5400]{1,0:T(8,128)} %param.12) | copy-start | bytes 1036804
  7.1 17.9 %copy-start.8 = (bf16[255,2700]{0,1:T(8,128)(2,1)S(1)}, bf16[255,2700]{0,1:T(8,128)(2,1)}, u32[]{:S(2)}) copy-start(bf16[255,2700]{0,1:T(8,128)(2,1)} %param.17) | copy-start | bytes 4131004
  21.5 13.8 %copy-start.1 = (f32[4,2,128,128]{3,2,1,0:T(8,128)S(1)}, f32[4,2,128,128]{3,2,1,0:T(8,128)}, u32[]{:S(2)}) copy-start(f32[4,2,128,128]{3,2,1,0:T(8,128)} %constant.90.clone.back_twist_ref) | copy-start | bytes 1572868
  21.6 13.8 %copy-start.3 = (bf16[4,96,384]{2,1,0:T(8,128)(2,1)S(1)}, bf16[4,96,384]{2,1,0:T(8,128)(2,1)}, u32[]{:S(2)}) copy-start(bf16[4,96,384]{2,1,0:T(8,128)(2,1)} %constant.89.clone.back_first_ref) | copy-start | bytes 884740
  23.4 10.6 %collective-permute-start.1 = (f16[16,5400]{1,0:T(8,128)(2,1)}, f16[16,5400]{1,0:T(8,128)(2,1)}, u32[]{:S(2)}, u32[]{:S(2)}) collective-permute-start(f16[16,5400]{1,0:T(8,128)(2,1)} %select_convert_fusion), channel_id=1, source_target_pairs={{0,1},{1,0},{2,3},{3,2},{4,5},{5,4},{6,7},{7,6},{8,9},{9,8},{10,11... | collective-permute-start | bytes 518408 | tf_op jit(solution)/shard_map/ppermute | solution.py:404
  31.6 3.7 %copy-start.2 = (bf16[4,128,288]{2,1,0:T(8,128)(2,1)S(1)}, bf16[4,128,288]{2,1,0:T(8,128)(2,1)}, u32[]{:S(2)}) copy-start(bf16[4,128,288]{2,1,0:T(8,128)(2,1)} %constant.86.clone.first_ref) | copy-start | bytes 884740
  31.6 3.8 %copy-start.4 = (f32[4,2,64,128]{3,2,1,0:T(8,128)S(1)}, f32[4,2,64,128]{3,2,1,0:T(8,128)}, u32[]{:S(2)}) copy-start(f32[4,2,64,128]{3,2,1,0:T(8,128)} %constant.87.clone.twist_ref) | copy-start | bytes 786436
  31.6 3.8 %copy-start.5 = (bf16[128,384]{1,0:T(8,128)(2,1)S(1)}, bf16[128,384]{1,0:T(8,128)(2,1)}, u32[]{:S(2)}) copy-start(bf16[128,384]{1,0:T(8,128)(2,1)} %constant.88.clone.second_ref) | copy-start | bytes 294916
  31.6 3.8 %copy-start.6 = (bf16[256,128]{1,0:T(8,128)(2,1)S(1)}, bf16[256,128]{1,0:T(8,128)(2,1)}, u32[]{:S(2)}) copy-start(bf16[256,128]{1,0:T(8,128)(2,1)} %constant.91.clone.back_second_ref) | copy-start | bytes 196612

commit v3 on v2

--- a/solution.py
+++ b/solution.py
@@ -191,7 +191,7 @@
     return jnp.where(lane < HALF, 1.0, -1.0)
 
 
-PIECES = ((0, 12), (12, 24), (24, 36), (36, 45))
+PIECES = 4
 
 
 def start_remote(src, dst, send, recv, axis, peer):
@@ -223,11 +223,13 @@
     out_ref,
     grid,
     parts,
+    routing,
     routed,
     model,
     leaving,
     columns,
     values,
+    window_rows,
     sums,
     leaving_sums,
     returned,
@@ -235,7 +237,6 @@
     wire_two,
     in_one,
     in_two,
-    keep,
     near,
     route_send,
     route_recv,
@@ -250,7 +251,7 @@
 ):
     me = lax.axis_index("lat")
     band = lax.axis_index("freq")
-    blocks = synth_ref.shape[0]
+    blocks = routing.shape[0]
     rows = re_ref.shape[0]
     deep = HALF // blocks
     total = rows * blocks
@@ -265,11 +266,15 @@
         pl.semaphore_signal(barrier, inc=1, device_id={"freq": peer}, device_id_type=pl.DeviceIdType.MESH)
     pl.semaphore_wait(barrier, blocks + 1)
 
+    slots = synth_ref.shape[0]
+    for part in range(2):
+        block = jnp.concatenate([synth_ref[:, part], jnp.zeros((CP - slots, total), jnp.float32)], axis=0).T
+        routing[:, part * rows : (part + 1) * rows] = block.reshape(blocks, rows, CP).astype(routing.dtype)
     routes = [
-        start_remote(synth_ref.at[peer], routed.at[me], route_send.at[d], route_recv.at[d], "lat", peer)
+        start_remote(routing.at[peer], routed.at[me], route_send.at[d], route_recv.at[d], "lat", peer)
         for d, peer in enumerate(peers)
     ]
-    own = pltpu.make_async_copy(synth_ref.at[me], routed.at[me], near)
+    own = pltpu.make_async_copy(routing.at[me], routed.at[me], near)
     own.start()
 
     grid[...] = jnp.zeros_like(grid)
@@ -316,6 +321,10 @@
     ]
     own = pltpu.make_async_copy(leaving.at[me], columns.at[me], near)
     own.start()
+    gap = jnp.zeros((kernel_ref.shape[0], HALF - NA), jnp.float32)
+    for j in range(deep):
+        piece = kernel_ref[:, j * NA : (j + 1) * NA]
+        window_rows[:, j] = jnp.concatenate([piece, gap, piece, gap], axis=1)
     own.wait()
     for copy in sent:
         copy.wait()
@@ -330,7 +339,7 @@
         def q_step(j, acc):
             q0 = j * qb
             base = q0 - p0 + total - rows
-            window = [kernel_ref[base + e] for e in range(rows + qb - 1)]
+            window = [window_rows[base + e] for e in range(rows + qb - 1)]
             terms = [values[q0 + q] for q in range(qb)]
             acc = list(acc)
             for p in range(rows):
@@ -358,6 +367,12 @@
     back_sine = back_twist_ref[band, 1]
     back_second = back_second_ref[...]
     parts[...] = returned[...].astype(jnp.float32)
+    even = 1.0 - lax.rem(band, 2).astype(jnp.float32)
+    keep_own = jnp.where((band == 1) | (band == 3), -1.0, 1.0)
+    keep_beside = jnp.where(band < 2, 1.0, -1.0)
+    give_beside = jnp.where((band == 1) | (band == 2), 1.0, -1.0)
+    step = rows // PIECES
+    ones = []
     for r in range(rows):
         held_sums = parts[:, r * deep : (r + 1) * deep].reshape(HALF, CP).astype(jnp.bfloat16)
         both = jnp.dot(
@@ -365,39 +380,35 @@
         )
         middle = both[:CP] * SCALE - pltpu.roll(both[CP:], HALF, 1) * sign
         turned = middle * back_cosine + pltpu.roll(middle, HALF, 1) * back_sine
-        grid[r] = lax.dot_general(
+        both = lax.dot_general(
             back_first, cols_of_three(turned), (((1,), (1,)), ((), ())), preferred_element_type=jnp.float32
         )
-
-    even = 1.0 - lax.rem(band, 2).astype(jnp.float32)
-    keep_own = jnp.where((band == 1) | (band == 3), -1.0, 1.0)
-    keep_beside = jnp.where(band < 2, 1.0, -1.0)
-    give_beside = jnp.where((band == 1) | (band == 2), 1.0, -1.0)
-    ones = []
-    for k, (low, high) in enumerate(PIECES):
-        for a in range(low, high):
-            real = grid[:, a]
-            wire_one[a] = real.astype(wire_one.dtype)
-            keep[a] = even * real + (1.0 - even) * grid[:, AP + a]
-        piece = pl.ds(low, high - low)
-        ones.append(
-            start_remote(wire_one.at[piece], in_one.at[piece], one_send.at[k], one_recv.at[k], "freq", beside)
-        )
+        real = both[:AP]
+        wire_one[r] = real.astype(wire_one.dtype)
+        grid[r, :AP] = even * real + (1.0 - even) * both[AP:]
+        if (r + 1) % step == 0:
+            k = r // step
+            piece = pl.ds(k * step, step)
+            ones.append(
+                start_remote(wire_one.at[piece], in_one.at[piece], one_send.at[k], one_recv.at[k], "freq", beside)
+            )
     twos = []
-    for k, (low, high) in enumerate(PIECES):
+    for k in range(PIECES):
         ones[k].wait()
-        piece = pl.ds(low, high - low)
-        chosen = keep[low:high]
-        arrived = in_one[low:high].astype(jnp.float32)
-        wire_two[low:high] = (chosen + give_beside * arrived).astype(wire_two.dtype)
-        keep[low:high] = keep_own * chosen + keep_beside * arrived
+        piece = pl.ds(k * step, step)
+        chosen = grid[piece, :AP]
+        arrived = in_one[piece].astype(jnp.float32)
+        wire_two[piece] = (chosen + give_beside * arrived).astype(wire_two.dtype)
+        grid[piece, :AP] = keep_own * chosen + keep_beside * arrived
         twos.append(
             start_remote(wire_two.at[piece], in_two.at[piece], two_send.at[k], two_recv.at[k], "freq", across)
         )
-    for k, (low, high) in enumerate(PIECES):
+    for k in range(PIECES):
         twos[k].wait()
-        for a in range(low, high):
-            out_ref[:, a * NC : (a + 1) * NC] = (keep[a] + in_two[a].astype(jnp.float32))[:, :NC]
+        piece = pl.ds(k * step, step)
+        grid[piece, :AP] = grid[piece, :AP] + in_two[piece].astype(jnp.float32)
+    for a in range(NA):
+        out_ref[:, a * NC : (a + 1) * NC] = grid[:, a, :NC]
 
 
 def swap(values, distance):
@@ -421,13 +432,16 @@
     across = swap(short, 2).astype(jnp.float32)
     added = gravity + across
     taken = jnp.where(lower, gravity - across, across - gravity)
-    beside = swap(jnp.where(even, taken, added).astype(jnp.float16), 1).astype(jnp.float32)
+    cut = slots // 2
+    lead = jnp.einsum("ocn,onq->ocq", coef[:cut], legendre[:cut], preferred_element_type=jnp.float32)
+    given = jnp.where(even, taken, added).astype(jnp.float16)
+    given, rest, lead = lax.optimization_barrier((given, coef[cut:], lead))
+    beside = swap(given, 1).astype(jnp.float32)
+    tail = jnp.einsum("ocn,onq->ocq", rest, legendre[cut:], preferred_element_type=jnp.float32)
+    synth = jnp.concatenate([lead, tail], axis=0)
     h_re = jnp.where(even, added + jnp.where(lower, beside, -beside), beside)
     h_im = jnp.where(even, 0.0, jnp.where(lower, -taken, taken))
 
-    synth = jnp.einsum("ocn,onq->ocq", coef, legendre, preferred_element_type=jnp.float32).astype(jnp.bfloat16)
-    synth = synth.reshape(slots, 2, blocks, rows).transpose(2, 1, 3, 0).reshape(blocks, 2 * rows, slots)
-    synth = jnp.pad(synth, ((0, 0), (0, 0), (0, CP - slots)))
     held = -(-(-(-order_table.shape[0] // 4) // NA) // 8) * 8
     mine = lax.dynamic_index_in_dim(order_table.reshape(blocks, 4, slots), band, 1, keepdims=False)
     place = mine // 4
@@ -438,9 +452,7 @@
 
     width = deep * NA
     padded = jnp.pad(kernel, ((0, 0), (0, width * blocks - kernel.shape[1])))
-    own = lax.dynamic_slice_in_dim(padded, block * width, width, 1).reshape(2 * total - 1, deep, NA)
-    own = jnp.pad(own, ((0, 0), (0, 0), (0, HALF - NA)))
-    own = jnp.concatenate([own, own], axis=2).astype(jnp.float32)
+    own = lax.dynamic_slice_in_dim(padded, block * width, width, 1).astype(jnp.float32)
 
     back_second = np.concatenate([second[:HALF].T, second[HALF:].T], axis=0)
     back_second = np.concatenate(numpy_pair(back_second), axis=1)
@@ -449,10 +461,10 @@
     back_first = three_cols(first.transpose(0, 2, 1))
 
     lanes = (blocks, rows * deep, CP)
-    line = (NA, rows, CP)
+    line = (rows, AP, CP)
     wire = jnp.bfloat16
     peers = pltpu.SemaphoreType.DMA((blocks - 1,))
-    pieces = pltpu.SemaphoreType.DMA((len(PIECES),))
+    pieces = pltpu.SemaphoreType.DMA((PIECES,))
     return pl.pallas_call(
         residual_kernel,
         out_shape=jax.ShapeDtypeStruct(gravity.shape, jnp.float32),
@@ -461,11 +473,13 @@
         scratch_shapes=[
             pltpu.VMEM((rows, 2 * AP, CP), jnp.float32),
             pltpu.VMEM(lanes, jnp.float32),
-            pltpu.VMEM(synth.shape, jnp.bfloat16),
+            pltpu.VMEM((blocks, 2 * rows, CP), jnp.bfloat16),
+            pltpu.VMEM((blocks, 2 * rows, CP), jnp.bfloat16),
             pltpu.VMEM((rows, held, CP), jnp.float32),
             pltpu.VMEM(lanes, wire),
             pltpu.VMEM(lanes, wire),
             pltpu.VMEM((total, deep, CP), jnp.float32),
+            pltpu.VMEM((2 * total - 1, deep, CP), jnp.float32),
             pltpu.VMEM((rows, deep, CP), jnp.float32),
             pltpu.VMEM((blocks - 1, rows * deep, CP), wire),
             pltpu.VMEM(lanes, wire),
@@ -473,7 +487,6 @@
             pltpu.VMEM(line, wire),
             pltpu.VMEM(line, wire),
             pltpu.VMEM(line, wire),
-            pltpu.VMEM(line, jnp.float32),
             pltpu.SemaphoreType.DMA,
             peers,
             peers,

time: 74.4 us -> 70.6 us (0.949)
  local copies, waits for them, and re-layouts: 10.5 us -> 4.29 us
  matrix products: 14.4 us -> 19.1 us
  Pallas kernels: 37.9 us -> 36.5 us
  other arithmetic: 5.47 us -> 4.57 us
    dot_general x1 -> x2, matrix products: 14.4 us -> 19.1 us  [the longest x1 9.87 us: band_device(): jnp.einsum('ocn,onq->ocq', coef[:cut], legendre[:cut], preferred_element_...]
    reshape x2 -> x0, local copies, waits for them, and re-layouts: 3.73 us -> none  [band_device(): lax.dynamic_slice_in_dim(padded, block * width, width, 1)]
    pad x2 -> x0, local copies, waits for them, and re-layouts: 2.08 us -> none  [the longest x1 1.15 us: band_device(): own = jnp.pad(own, ((0, 0), (0, 0), (0, HALF - NA)))]
    unnamed x21 -> x22, local copies, waits for them, and re-layouts: 0.79 us -> 2.47 us
    transpose x1 -> x0, local copies, waits for them, and re-layouts: 1.46 us -> none  [band_device(): synth.reshape(slots, 2, blocks, rows).transpose(2, 1, 3, 0)]
    pallas_call x1, Pallas kernels: 37.9 us -> 36.5 us  [band_device(): pl.pallas_call(residual_kernel, out_shape=jax.ShapeDtypeStruct(gravity.sh...]
    slice x0 -> x1, local copies, waits for them, and re-layouts: none -> 0.92 us  [band_device(): given, rest, lead = lax.optimization_barrier((given, coef[cut:], lead))]
    dynamic_slice x1 -> x0, local copies, waits for them, and re-layouts: 0.77 us -> none  [band_device(): lax.dynamic_slice_in_dim(padded, block * width, width, 1)]
where the time goes in v3:
time: 70.6 us; the launch traced here: 70.3 us
  Pallas kernels  36.5 us (52%)
  matrix products  19.1 us (27%)
  starting transfers between devices  5.68 us (8%)
  other arithmetic  4.57 us (6%)
  local copies, waits for them, and re-layouts  4.29 us (6%)
    pallas_call x1, Pallas kernels, band_device(): pl.pallas_call(residual_kernel, out_shape=jax.ShapeDtypeStruct(gravity.sh...  36.5 us
    dot_general x1, matrix products, band_device(): jnp.einsum('ocn,onq->ocq', coef[:cut], legendre[:cut], preferred_element_...  9.87 us
    dot_general x1, matrix products, band_device(): jnp.einsum('ocn,onq->ocq', rest, legendre[cut:], preferred_element_type=j...  9.19 us
    ppermute x2, starting transfers between devices, swap(): return lax.ppermute(values, 'freq', [(f, f ^ distance) for f in range(4)])  5.68 us
    unnamed x22, local copies, waits for them, and re-layouts  2.47 us
    convert_element_type x1, other arithmetic, band_device(): short = gravity.astype(jnp.float16)  1.67 us
  transfers between devices with their start and end apart: 2, of which 0 were waited for; matrix products, arithmetic and copies ran while one was open for 33% of the time, Pallas kernels for 0%

profile of v3, /device:TPU:0, one launch (start us, length us, event | category | flops | bytes accessed | tf_op | source)
XLA Modules:
  0.0 70.3 jit_solution(5435031851845232671)
XLA Ops:
  0.0 1.7 %convert_element_type.23 = f16[16,5400]{1,0:T(8,128)(2,1)} convert(f32[16,5400]{1,0:T(8,128)} %param.12) | non-fusion elementwise | flops 86400 | bytes 518400 | tf_op jit(solution)/shard_map/convert_element_type | solution.py:431
  1.7 4.0 %collective-permute-start = (f16[16,5400]{1,0:T(8,128)(2,1)}, f16[16,5400]{1,0:T(8,128)(2,1)}, u32[]{:S(2)}, u32[]{:S(2)}) collective-permute-start(f16[16,5400]{1,0:T(8,128)(2,1)} %convert_element_type.23), channel_id=1, source_target_pairs={{0,2},{1,3},{2,0},{3,1},{4,6},{5,7},{6,4},{7,5},{8,10},{9,11},{10,... | collective-permute-start | bytes 518408 | tf_op jit(solution)/shard_map/ppermute | solution.py:415
  5.7 0.8 %reshape.7 = s32[8,4,68]{2,1,0:T(4,128)S(1)} reshape(s32[2176]{0:T(1024)} %param.15) | data formatting | bytes 17408 | tf_op jit(solution)/shard_map/reshape | solution.py:446
  6.6 0.4 fusion.4.select_ref
  7.0 0.0 copy-start.9
  7.0 0.0 copy-start.7
  7.0 9.9 %fusion.2 = f32[34,2,128]{2,1,0:T(2,128)} fusion(bf16[68,2,2176]{2,1,0:T(2,128)(2,1)} %param.13, bf16[68,2176,128]{2,1,0:T(8,128)(2,1)} %param.14), kind=kOutput, calls=%fused_computation.2 | convolution fusion | flops 37879808 | bytes 19566592 | tf_op jit(solution)/shard_map/ocn,onq->ocq/dot_general | solution.py:436
  17.0 0.9 %slice.12 = bf16[34,2,2176]{2,1,0:T(2,128)(2,1)} slice(bf16[68,2,2176]{2,1,0:T(2,128)(2,1)S(1)} %copy-done.7), slice={[34:68], [0:2], [0:2176]} | slice | bytes 591872 | tf_op jit(solution)/shard_map/slice | solution.py:438
  17.9 1.7 %copy.14 = bf16[255,2700]{1,0:T(8,128)(2,1)S(1)} copy(bf16[255,2700]{0,1:T(8,128)(2,1)} %param.17) | data formatting | bytes 2754000 | tf_op args[5]
  19.5 0.1 fusion.8.kernel_ref
  19.7 0.0 copy-start.6
  19.7 1.2 %select_convert_fusion = f16[16,5400]{1,0:T(8,128)(2,1)S(1)} fusion(f32[16,5400]{1,0:T(8,128)} %param.12, f16[16,5400]{1,0:T(8,128)(2,1)} %collective-permute-done, pred[]{:T(512)S(6)} %lt.21, pred[]{:T(512)S(6)} %eq.20), kind=kLoop, calls=%fused_computation.16 | loop fusion | flops 604800 | bytes 691202 | tf_op jit(solution)/shard_map/convert_element_type | solution.py:437
  20.9 0.0 copy-start
  20.9 0.0 copy-start.1
  20.9 0.0 copy-start.2
  20.9 0.0 copy-start.3
  21.0 0.0 copy-start.4
  21.0 0.0 copy-start.5
  21.0 1.6 %collective-permute-start.1 = (f16[16,5400]{1,0:T(8,128)(2,1)S(1)}, f16[16,5400]{1,0:T(8,128)(2,1)S(1)}, u32[]{:S(2)}, u32[]{:S(2)}) collective-permute-start(f16[16,5400]{1,0:T(8,128)(2,1)S(1)} %select_convert_fusion), channel_id=1, source_target_pairs={{0,1},{1,0},{2,3},{3,2},{4,5},{5,4},{6,7},{7,6},{8,9},{9,8},{10,11... | collective-permute-start | bytes 518408 | tf_op jit(solution)/shard_map/ppermute | solution.py:415
  22.6 9.2 %fusion = f32[34,2,128]{2,1,0:T(2,128)S(1)} fusion(bf16[34,2,2176]{2,1,0:T(2,128)(2,1)} %slice.12, bf16[68,2176,128]{2,1,0:T(8,128)(2,1)} %param.14), kind=kOutput, calls=%fused_computation | convolution fusion | flops 37879808 | bytes 19270656 | tf_op jit(solution)/shard_map/ocn,onq->ocq/dot_general | solution.py:440
  31.9 1.1 %fusion.7 = (f32[16,5400]{1,0:T(8,128)S(1)}, f32[16,5400]{1,0:T(8,128)S(1)}) fusion(f32[16,5400]{1,0:T(8,128)S(1)} %copy-done.6, f16[16,5400]{1,0:T(8,128)(2,1)} %collective-permute-done, pred[]{:T(512)S(6)} %lt.21, pred[]{:T(512)S(6)} %eq.20, f16[16,5400]{1,0:T(8,128)(2,1)S(1)} %collective-permute-done.1), kind=kLoop, calls=%fused_computation.15 | loop fusion | flops 1123200 | bytes 1382402 | tf_op jit(solution)/shard_map/jit(_where)/select_n | solution.py:443
  33.0 0.1 broadcast_in_dim.7.weight_ref
  33.1 36.5 %residual_band.1 = f32[16,5400]{1,0:T(8,128)S(1)} custom-call(f32[16,5400]{1,0:T(8,128)S(1)} %get-tuple-element.12.re_ref, f32[16,5400]{1,0:T(8,128)S(1)} %get-tuple-element.11.im_ref, f32[68,2,128]{2,1,0:T(2,128)S(1)} %pad_maximum_fusion.synth_ref, bf16[8,128,1024]{2,1,0:T(8,128)(2,1)S(1)} %fusion.4.select_ref, ...), custom_call_target="tpu_custom_call" | custom-call | tf_op jit(solution)/shard_map/residual_band/pallas_call | solution.py:468
  69.6 0.7 %copy.16 = f32[16,5400]{1,0:T(8,128)} copy(f32[16,5400]{1,0:T(8,128)S(1)} %residual_band.1) | data formatting | bytes 691200
  (18 shorter events, 0.2 us)
Async XLA Ops:
  1.7 18.1 %collective-permute-start = (f16[16,5400]{1,0:T(8,128)(2,1)}, f16[16,5400]{1,0:T(8,128)(2,1)}, u32[]{:S(2)}, u32[]{:S(2)}) collective-permute-start(f16[16,5400]{1,0:T(8,128)(2,1)} %convert_element_type.23), channel_id=1, source_target_pairs={{0,2},{1,3},{2,0},{3,1},{4,6},{5,7},{6,4},{7,5},{8,10},{9,11},{10,... | collective-permute-start | bytes 518408 | tf_op jit(solution)/shard_map/ppermute | solution.py:415
  7.0 9.9 %copy-start.9 = (s32[16]{0:T(128)S(1)}, s32[16]{0:T(128)}, u32[]{:S(2)}) copy-start(s32[16]{0:T(128)} %param.16) | copy-start | bytes 196
  7.0 9.9 %copy-start.7 = (bf16[68,2,2176]{2,1,0:T(2,128)(2,1)S(1)}, bf16[68,2,2176]{2,1,0:T(2,128)(2,1)}, u32[]{:S(2)}) copy-start(bf16[68,2,2176]{2,1,0:T(2,128)(2,1)} %param.13) | copy-start | bytes 1775620
  19.7 12.1 %copy-start.8 = (f32[34,2,128]{2,1,0:T(2,128)S(1)}, f32[34,2,128]{2,1,0:T(2,128)}, u32[]{:S(2)}) copy-start(f32[34,2,128]{2,1,0:T(2,128)} %fusion.2) | copy-start | bytes 104452
  19.7 12.2 %copy-start.6 = (f32[16,5400]{1,0:T(8,128)S(1)}, f32[16,5400]{1,0:T(8,128)}, u32[]{:S(2)}) copy-start(f32[16,5400]{1,0:T(8,128)} %param.12) | copy-start | bytes 1036804
  20.9 12.1 %copy-start = (f32[4,2,128,128]{3,2,1,0:T(8,128)S(1)}, f32[4,2,128,128]{3,2,1,0:T(8,128)}, u32[]{:S(2)}) copy-start(f32[4,2,128,128]{3,2,1,0:T(8,128)} %constant.90.clone.back_twist_ref) | copy-start | bytes 1572868
  20.9 12.1 %copy-start.1 = (bf16[4,128,288]{2,1,0:T(8,128)(2,1)S(1)}, bf16[4,128,288]{2,1,0:T(8,128)(2,1)}, u32[]{:S(2)}) copy-start(bf16[4,128,288]{2,1,0:T(8,128)(2,1)} %constant.86.clone.first_ref) | copy-start | bytes 884740
  20.9 12.1 %copy-start.2 = (bf16[4,96,384]{2,1,0:T(8,128)(2,1)S(1)}, bf16[4,96,384]{2,1,0:T(8,128)(2,1)}, u32[]{:S(2)}) copy-start(bf16[4,96,384]{2,1,0:T(8,128)(2,1)} %constant.89.clone.back_first_ref) | copy-start | bytes 884740
  20.9 12.1 %copy-start.3 = (f32[4,2,64,128]{3,2,1,0:T(8,128)S(1)}, f32[4,2,64,128]{3,2,1,0:T(8,128)}, u32[]{:S(2)}) copy-start(f32[4,2,64,128]{3,2,1,0:T(8,128)} %constant.87.clone.twist_ref) | copy-start | bytes 786436
  21.0 12.1 %copy-start.4 = (bf16[128,384]{1,0:T(8,128)(2,1)S(1)}, bf16[128,384]{1,0:T(8,128)(2,1)}, u32[]{:S(2)}) copy-start(bf16[128,384]{1,0:T(8,128)(2,1)} %constant.88.clone.second_ref) | copy-start | bytes 294916
  21.0 12.1 %copy-start.5 = (bf16[256,128]{1,0:T(8,128)(2,1)S(1)}, bf16[256,128]{1,0:T(8,128)(2,1)}, u32[]{:S(2)}) copy-start(bf16[256,128]{1,0:T(8,128)(2,1)} %constant.91.clone.back_second_ref) | copy-start | bytes 196612
  21.0 10.9 %collective-permute-start.1 = (f16[16,5400]{1,0:T(8,128)(2,1)S(1)}, f16[16,5400]{1,0:T(8,128)(2,1)S(1)}, u32[]{:S(2)}, u32[]{:S(2)}) collective-permute-start(f16[16,5400]{1,0:T(8,128)(2,1)S(1)} %select_convert_fusion), channel_id=1, source_target_pairs={{0,1},{1,0},{2,3},{3,2},{4,5},{5,4},{6,7},{7,6},{8,9},{9,8},{10,11... | collective-permute-start | bytes 518408 | tf_op jit(solution)/shard_map/ppermute | solution.py:415

commit v4 on v3

--- a/solution.py
+++ b/solution.py
@@ -411,6 +411,31 @@
         out_ref[:, a * NC : (a + 1) * NC] = grid[:, a, :NC]
 
 
+def synthesis_kernel(coef_ref, legendre_ref, out_ref):
+    for k in range(out_ref.shape[0]):
+        out_ref[k] = jnp.dot(coef_ref[k], legendre_ref[k], preferred_element_type=jnp.float32)
+
+
+def synthesis(coef, legendre, start, count):
+    _, degrees, rows = legendre.shape
+    step = 4
+    return pl.pallas_call(
+        synthesis_kernel,
+        grid=(count // step,),
+        out_shape=jax.ShapeDtypeStruct((count, 2, rows), jnp.float32),
+        in_specs=[
+            pl.BlockSpec((step, 2, degrees), lambda i: (i + start // step, 0, 0)),
+            pl.BlockSpec((step, degrees, rows), lambda i: (i + start // step, 0, 0)),
+        ],
+        out_specs=pl.BlockSpec((step, 2, rows), lambda i: (i, 0, 0)),
+        compiler_params=pltpu.CompilerParams(vmem_limit_bytes=24 * 2**20),
+        cost_estimate=pl.CostEstimate(
+            flops=4 * count * degrees * rows, bytes_accessed=2 * count * degrees * (rows + 2), transcendentals=0
+        ),
+        name="synthesis",
+    )(coef, legendre)
+
+
 def swap(values, distance):
     return lax.ppermute(values, "freq", [(f, f ^ distance) for f in range(4)])
 
@@ -432,12 +457,12 @@
     across = swap(short, 2).astype(jnp.float32)
     added = gravity + across
     taken = jnp.where(lower, gravity - across, across - gravity)
-    cut = slots // 2
-    lead = jnp.einsum("ocn,onq->ocq", coef[:cut], legendre[:cut], preferred_element_type=jnp.float32)
+    cut = slots // 8 * 4 + 4
+    lead = synthesis(coef, legendre, 0, cut)
     given = jnp.where(even, taken, added).astype(jnp.float16)
-    given, rest, lead = lax.optimization_barrier((given, coef[cut:], lead))
+    given, rest, lead = lax.optimization_barrier((given, coef, lead))
     beside = swap(given, 1).astype(jnp.float32)
-    tail = jnp.einsum("ocn,onq->ocq", rest, legendre[cut:], preferred_element_type=jnp.float32)
+    tail = synthesis(rest, legendre, cut, slots - cut)
     synth = jnp.concatenate([lead, tail], axis=0)
     h_re = jnp.where(even, added + jnp.where(lower, beside, -beside), beside)
     h_im = jnp.where(even, 0.0, jnp.where(lower, -taken, taken))
@@ -520,7 +545,7 @@
 
 
 def fits(mesh):
-    return mesh.shape["freq"] == 4 and HALF % mesh.shape["lat"] == 0
+    return mesh.shape["freq"] == 4 and HALF % mesh.shape["lat"] == 0 and mesh.shape["lat"] == 8
 
 
 def solution(mesh):

time: 70.6 us -> 69.3 us (0.982)
  Pallas kernels: 36.5 us -> 56.7 us
  matrix products: 19.1 us -> 0 us
  other arithmetic: 4.57 us -> 1.9 us
    pallas_call x0 -> x2, Pallas kernels: none -> 20.2 us  [synthesis(): pl.pallas_call(synthesis_kernel, grid=(count // step,), out_shape=jax.Sha...]
    dot_general x2 -> x0, matrix products: 19.1 us -> none  [the longest x1 9.87 us: band_device(): jnp.einsum('ocn,onq->ocq', coef[:cut], legendre[:cut], preferred_element_...]
    convert_element_type x1, other arithmetic: 1.16 us -> 0.09 us  [band_device(): given = jnp.where(even, taken, added).astype(jnp.float16)]
    unnamed x22, local copies, waits for them, and re-layouts: 2.47 us -> 3.41 us
    select_n x1, other arithmetic: 1.08 us -> 0.16 us  [band_device(): h_im = jnp.where(even, 0.0, jnp.where(lower, -taken, taken))]
    slice x1 -> x0, local copies, waits for them, and re-layouts: 0.92 us -> none  [band_device(): given, rest, lead = lax.optimization_barrier((given, coef[cut:], lead))]
  transfers between devices with their start and end apart: 2 -> 2, of which waited for: 0 -> 0; matrix products, arithmetic and copies ran while one was open for 33% -> 6% of each run, Pallas kernels for 0% -> 29%
where the time goes in v4:
time: 69.3 us; the launch traced here: 68.9 us
  Pallas kernels  56.7 us (82%)
  starting transfers between devices  5.74 us (8%)
  local copies, waits for them, and re-layouts  4.31 us (6%)
  other arithmetic  1.9 us (3%)
    pallas_call x1, Pallas kernels, band_device(): pl.pallas_call(residual_kernel, out_shape=jax.ShapeDtypeStruct(gravity.sh...  36.5 us
    pallas_call x2, Pallas kernels, synthesis(): pl.pallas_call(synthesis_kernel, grid=(count // step,), out_shape=jax.Sha...  20.2 us
    ppermute x2, starting transfers between devices, swap(): return lax.ppermute(values, 'freq', [(f, f ^ distance) for f in range(4)])  5.74 us
    unnamed x22, local copies, waits for them, and re-layouts  3.41 us
  transfers between devices with their start and end apart: 2, of which 0 were waited for; matrix products, arithmetic and copies ran while one was open for 6% of the time, Pallas kernels for 29%

profile of v4, /device:TPU:0, one launch (start us, length us, event | category | flops | bytes accessed | tf_op | source)
XLA Modules:
  0.0 68.9 jit_solution(12050396981318646462)
XLA Ops:
  0.0 1.0 %convert_element_type.23 = f16[16,5400]{1,0:T(8,128)(2,1)S(1)} convert(f32[16,5400]{1,0:T(8,128)} %param.12) | non-fusion elementwise | flops 86400 | bytes 518400 | tf_op jit(solution)/shard_map/convert_element_type | solution.py:456
  1.0 4.1 %collective-permute-start = (f16[16,5400]{1,0:T(8,128)(2,1)S(1)}, f16[16,5400]{1,0:T(8,128)(2,1)S(1)}, u32[]{:S(2)}, u32[]{:S(2)}) collective-permute-start(f16[16,5400]{1,0:T(8,128)(2,1)S(1)} %convert_element_type.23), channel_id=1, source_target_pairs={{0,2},{1,3},{2,0},{3,1},{4,6},{5,7},{6,4},{7,5},{8,10},{9,11},{10,... | collective-permute-start | bytes 518408 | tf_op jit(solution)/shard_map/ppermute | solution.py:440
  5.1 0.8 %reshape.7 = s32[8,4,68]{2,1,0:T(4,128)S(1)} reshape(s32[2176]{0:T(1024)} %param.15) | data formatting | bytes 17408 | tf_op jit(solution)/shard_map/reshape | solution.py:471
  6.0 0.0 copy-start
  6.0 2.6 %copy.14 = bf16[255,2700]{1,0:T(8,128)(2,1)} copy(bf16[255,2700]{0,1:T(8,128)(2,1)} %param.17) | data formatting | bytes 2754000 | tf_op args[5]
  8.6 0.4 fusion.select_ref
  9.0 0.0 copy-start.9
  9.0 0.0 copy-start.8
  9.0 10.8 %synthesis.2 = f32[36,2,128]{2,1,0:T(2,128)S(1)} custom-call(bf16[68,2,2176]{2,1,0:T(2,128)(2,1)S(1)} %copy-done, bf16[68,2176,128]{2,1,0:T(8,128)(2,1)} %legendre_ref.3), custom_call_target="tpu_custom_call" | custom-call | flops 40108032 | bytes 20367360 | tf_op jit(solution)/shard_map/synthesis/pallas_call | solution.py:422
  19.9 0.0 collective-permute-done
  19.9 0.1 select_convert_fusion
  20.0 1.6 %collective-permute-start.1 = (f16[16,5400]{1,0:T(8,128)(2,1)S(1)}, f16[16,5400]{1,0:T(8,128)(2,1)S(1)}, u32[]{:S(2)}, u32[]{:S(2)}) collective-permute-start(f16[16,5400]{1,0:T(8,128)(2,1)S(1)} %select_convert_fusion), channel_id=1, source_target_pairs={{0,1},{1,0},{2,3},{3,2},{4,5},{5,4},{6,7},{7,6},{8,9},{9,8},{10,11... | collective-permute-start | bytes 518408 | tf_op jit(solution)/shard_map/ppermute | solution.py:440
  21.6 0.1 fusion.4.kernel_ref
  21.8 0.0 copy-start.1
  21.8 0.0 copy-start.2
  21.8 0.0 copy-start.3
  21.8 0.0 copy-start.4
  21.8 0.0 copy-start.5
  21.8 0.0 copy-start.6
  21.9 9.5 %synthesis.3 = f32[32,2,128]{2,1,0:T(2,128)S(1)} custom-call(bf16[68,2,2176]{2,1,0:T(2,128)(2,1)S(1)} %copy-done, bf16[68,2176,128]{2,1,0:T(8,128)(2,1)} %legendre_ref.3), custom_call_target="tpu_custom_call" | custom-call | flops 35651584 | bytes 18104320 | tf_op jit(solution)/shard_map/synthesis/pallas_call | solution.py:422
  31.4 0.2 fusion.3
  31.6 0.1 broadcast_in_dim.7.weight_ref
  31.7 36.5 %residual_band.1 = f32[16,5400]{1,0:T(8,128)S(1)} custom-call(f32[16,5400]{1,0:T(8,128)S(1)} %get-tuple-element.12.re_ref, f32[16,5400]{1,0:T(8,128)S(1)} %get-tuple-element.11.im_ref, f32[68,2,128]{2,1,0:T(2,128)S(1)} %pad_maximum_fusion.synth_ref, bf16[8,128,1024]{2,1,0:T(8,128)(2,1)S(1)} %fusion.select_ref, f32[16,1,128]{2,1,0:T(1,128)S(1)} %broadcast_in_dim.7.weight_ref, ...), custom_call_target="tpu_custom_call" | custom-call | tf_op jit(solution)/shard_map/residual_band/pallas_call | solution.py:493
  68.2 0.7 %copy.16 = f32[16,5400]{1,0:T(8,128)} copy(f32[16,5400]{1,0:T(8,128)S(1)} %residual_band.1) | data formatting | bytes 691200
  (17 shorter events, 0.1 us)
Async XLA Ops:
  1.0 18.9 %collective-permute-start = (f16[16,5400]{1,0:T(8,128)(2,1)S(1)}, f16[16,5400]{1,0:T(8,128)(2,1)S(1)}, u32[]{:S(2)}, u32[]{:S(2)}) collective-permute-start(f16[16,5400]{1,0:T(8,128)(2,1)S(1)} %convert_element_type.23), channel_id=1, source_target_pairs={{0,2},{1,3},{2,0},{3,1},{4,6},{5,7},{6,4},{7,5},{8,10},{9,11},{10,... | collective-permute-start | bytes 518408 | tf_op jit(solution)/shard_map/ppermute | solution.py:440
  6.0 3.0 %copy-start = (bf16[68,2,2176]{2,1,0:T(2,128)(2,1)S(1)}, bf16[68,2,2176]{2,1,0:T(2,128)(2,1)}, u32[]{:S(2)}) copy-start(bf16[68,2,2176]{2,1,0:T(2,128)(2,1)} %coef_ref.2) | copy-start | bytes 1775620
  9.0 10.8 %copy-start.9 = (s32[16]{0:T(128)S(1)}, s32[16]{0:T(128)}, u32[]{:S(2)}) copy-start(s32[16]{0:T(128)} %param.16) | copy-start | bytes 196
  9.0 10.9 %copy-start.8 = (f32[16,5400]{1,0:T(8,128)S(1)}, f32[16,5400]{1,0:T(8,128)}, u32[]{:S(2)}) copy-start(f32[16,5400]{1,0:T(8,128)} %param.12) | copy-start | bytes 1036804
  9.0 12.6 %copy-start.7 = (bf16[255,2700]{1,0:T(8,128)(2,1)S(1)}, bf16[255,2700]{1,0:T(8,128)(2,1)}, u32[]{:S(2)}) copy-start(bf16[255,2700]{1,0:T(8,128)(2,1)} %copy.14) | copy-start | bytes 4131004
  20.0 11.4 %collective-permute-start.1 = (f16[16,5400]{1,0:T(8,128)(2,1)S(1)}, f16[16,5400]{1,0:T(8,128)(2,1)S(1)}, u32[]{:S(2)}, u32[]{:S(2)}) collective-permute-start(f16[16,5400]{1,0:T(8,128)(2,1)S(1)} %select_convert_fusion), channel_id=1, source_target_pairs={{0,1},{1,0},{2,3},{3,2},{4,5},{5,4},{6,7},{7,6},{8,9},{9,8},{10,11... | collective-permute-start | bytes 518408 | tf_op jit(solution)/shard_map/ppermute | solution.py:440
  21.8 9.8 %copy-start.1 = (f32[4,2,128,128]{3,2,1,0:T(8,128)S(1)}, f32[4,2,128,128]{3,2,1,0:T(8,128)}, u32[]{:S(2)}) copy-start(f32[4,2,128,128]{3,2,1,0:T(8,128)} %constant.90.clone.back_twist_ref) | copy-start | bytes 1572868
  21.8 9.8 %copy-start.2 = (bf16[4,128,288]{2,1,0:T(8,128)(2,1)S(1)}, bf16[4,128,288]{2,1,0:T(8,128)(2,1)}, u32[]{:S(2)}) copy-start(bf16[4,128,288]{2,1,0:T(8,128)(2,1)} %constant.86.clone.first_ref) | copy-start | bytes 884740
  21.8 9.8 %copy-start.3 = (bf16[4,96,384]{2,1,0:T(8,128)(2,1)S(1)}, bf16[4,96,384]{2,1,0:T(8,128)(2,1)}, u32[]{:S(2)}) copy-start(bf16[4,96,384]{2,1,0:T(8,128)(2,1)} %constant.89.clone.back_first_ref) | copy-start | bytes 884740
  21.8 9.8 %copy-start.4 = (f32[4,2,64,128]{3,2,1,0:T(8,128)S(1)}, f32[4,2,64,128]{3,2,1,0:T(8,128)}, u32[]{:S(2)}) copy-start(f32[4,2,64,128]{3,2,1,0:T(8,128)} %constant.87.clone.twist_ref) | copy-start | bytes 786436
  21.8 9.8 %copy-start.5 = (bf16[128,384]{1,0:T(8,128)(2,1)S(1)}, bf16[128,384]{1,0:T(8,128)(2,1)}, u32[]{:S(2)}) copy-start(bf16[128,384]{1,0:T(8,128)(2,1)} %constant.88.clone.second_ref) | copy-start | bytes 294916
  21.8 9.8 %copy-start.6 = (bf16[256,128]{1,0:T(8,128)(2,1)S(1)}, bf16[256,128]{1,0:T(8,128)(2,1)}, u32[]{:S(2)}) copy-start(bf16[256,128]{1,0:T(8,128)(2,1)} %constant.91.clone.back_second_ref) | copy-start | bytes 196612
